TPU v7x, 32 devices: a whole 2x2x4 slice. The times are simulated.
32 devices in a mesh: row: 32 (over z, y, x, core), col: 1.
Axes of the slice: x: 2, y: 2, z: 4, core: 2. Of those that a mesh axis runs over, the one named last changes fastest.
Arguments:
- inputs: bfloat16 [128, 128, 256], P('row', 'col'), may hold values from -6 to 6
- preactivation: bfloat16 [128, 128, 256], P('row', 'col'), may hold values from -6 to 6
- cotangent: bfloat16 [128, 128, 256], P('row', 'col'), may hold values from -6 to 6
- spectral: bfloat16 [2, 128, 64, 5, 1024], P(None, 'row', 'col'), may hold values from -2 to 2
- bypass: bfloat16 [32, 32], replicated, may hold values from -1 to 1
Outputs:
- grad_inputs: bfloat16 [128, 128, 256], P('row', 'col')
- grad_spectral: float32 [2, 128, 64, 5, 1024], P(None, 'row', 'col')
- grad_bypass: float32 [32, 32], replicated
All inputs are finite; a program needn't handle non-finite values.
Results may differ from a plain program's by a relative error of at most 0.022.
Values may be sent and summed in bfloat16 or wider, within the bound.
No kernel may reach another device: no remote copies, remote signals or barrier semaphores. Data moves between devices by JAX's collectives and lax.ppermute only.
A program may use at most 128 MiB of HBM per device.

v0:
```python
import math

import jax
import jax.numpy as jnp
from jax import lax
from jax.sharding import PartitionSpec as P

exact_mode = lax.Precision.HIGHEST


def counting(length):
    return jnp.arange(length, dtype=jnp.int32)


def kept_freq(slot_index, keep_count):
    return jnp.where(slot_index < keep_count // 2, slot_index, slot_index - keep_count)


def phase_table(outer_index, inner_index, length, direction):
    turn_count = jnp.mod(outer_index[:, None] * inner_index[None, :], length)
    angles = turn_count.astype(jnp.float32) * (2.0 * math.pi / length)
    cosine = jnp.cos(angles)
    sine_part = direction * jnp.sin(angles)
    top_rows = jnp.stack([cosine, -sine_part], axis=1)
    low_rows = jnp.stack([sine_part, cosine], axis=1)
    return jnp.stack([top_rows, low_rows], axis=0)


def time_forward(step_count, time_modes):
    turn_count = jnp.mod(counting(step_count)[:, None] * counting(time_modes)[None, :], step_count)
    angles = turn_count.astype(jnp.float32) * (2.0 * math.pi / step_count)
    return jnp.stack([jnp.cos(angles), -jnp.sin(angles)], axis=1)


def time_inverse(step_count, time_modes):
    turn_count = jnp.mod(counting(time_modes)[:, None] * counting(step_count)[None, :], step_count)
    angles = turn_count.astype(jnp.float32) * (2.0 * math.pi / step_count)
    return jnp.stack([jnp.cos(angles), -jnp.sin(angles)], axis=0)


def gelu_slope(values):
    normal_cdf = 0.5 * (1.0 + lax.erf(values * (1.0 / math.sqrt(2.0))))
    density = jnp.exp(-0.5 * values * values) * (1.0 / math.sqrt(2.0 * math.pi))
    return normal_cdf + values * density


def mix_modes(modes_in, modes_grad, weight, factor):
    in_real = modes_in[:, 0]
    in_imag = modes_in[:, 1]
    grad_real = modes_grad[:, 0]
    grad_imag = modes_grad[:, 1]
    real_part = factor * (
        in_real[..., :, None] * grad_real[..., None, :]
        + in_imag[..., :, None] * grad_imag[..., None, :]
    )
    imag_part = factor * (
        in_real[..., :, None] * grad_imag[..., None, :]
        - in_imag[..., :, None] * grad_real[..., None, :]
    )
    weight_grad = jnp.stack([real_part, imag_part], axis=0)
    w_real = weight[0]
    w_imag = weight[1]
    back_real = factor * (
        jnp.einsum("kyscd,kysd->kysc", w_real, grad_real, precision=exact_mode)
        + jnp.einsum("kyscd,kysd->kysc", w_imag, grad_imag, precision=exact_mode)
    )
    back_imag = factor * (
        jnp.einsum("kyscd,kysd->kysc", w_real, grad_imag, precision=exact_mode)
        - jnp.einsum("kyscd,kysd->kysc", w_imag, grad_real, precision=exact_mode)
    )
    return (weight_grad, jnp.stack([back_real, back_imag], axis=1))


def local(inputs, preactivation, cotangent, spectral, bypass):
    row_count, col_count, packed = inputs.shape
    chan_count = bypass.shape[0]
    step_count = packed // chan_count
    time_modes = spectral.shape[3]
    owned_row_modes = spectral.shape[1]
    owned_col_modes = spectral.shape[2]
    row_parts = lax.axis_size("row")
    col_parts = lax.axis_size("col")
    row_modes = owned_row_modes * row_parts
    col_modes = owned_col_modes * col_parts
    total_x = row_count * row_parts
    total_y = col_count * col_parts
    factor = 1.0 / math.sqrt(
        float(total_x * total_y * step_count * row_modes * col_modes * time_modes)
    )
    row_start = lax.axis_index("row") * row_count
    col_start = lax.axis_index("col") * col_count
    mode_width = owned_col_modes * time_modes * chan_count
    slopes = gelu_slope(preactivation.astype(jnp.float32))
    pre_grad = (cotangent.astype(jnp.float32) * slopes).astype(jnp.bfloat16)
    flat_inputs = inputs.reshape(-1, chan_count)
    flat_grad = pre_grad.reshape(-1, chan_count)
    local_bypass = jnp.einsum(
        "nc,nd->cd", flat_inputs, flat_grad, preferred_element_type=jnp.float32
    )
    bypass_total = lax.psum(local_bypass, ("row", "col"))
    grad_bypass = bypass_total * (1.0 / math.sqrt(float(total_x * total_y * step_count)))
    forward_t = time_forward(step_count, time_modes)
    col_table = phase_table(counting(col_modes), col_start + counting(col_count), total_y, -1.0)

    def column_terms(field):
        cube_view = field.astype(jnp.float32).reshape(row_count, col_count, step_count, chan_count)
        in_time = jnp.einsum("rytc,tqs->ryqsc", cube_view, forward_t, precision=exact_mode)
        return jnp.einsum("akpy,rypsc->raksc", col_table, in_time, precision=exact_mode)

    col_in, col_grad = (
        lax.psum_scatter(
            column_terms(inputs).astype(jnp.bfloat16), "col", scatter_dimension=2, tiled=True
        ).astype(jnp.float32),
        lax.psum_scatter(
            column_terms(pre_grad).astype(jnp.bfloat16), "col", scatter_dimension=2, tiled=True
        ).astype(jnp.float32),
    )
    flat_in = col_in.reshape(row_count, 2, mode_width)
    flat_cols = col_grad.reshape(row_count, 2, mode_width)
    stacked = jnp.stack([flat_in, flat_cols], axis=2)
    frequencies = kept_freq(counting(owned_row_modes * lax.axis_size("row")), row_modes)
    phases = phase_table(frequencies, row_start + counting(row_count), total_x, -1.0)
    owned_modes = lax.psum_scatter(
        jnp.einsum("akpr,rpbm->kabm", phases, stacked, precision=exact_mode),
        "row",
        scatter_dimension=0,
        tiled=True,
    )
    modes_in = owned_modes[:, :, 0]
    modes_grad = owned_modes[:, :, 1]
    mode_shape = (owned_row_modes, 2, owned_col_modes, time_modes, chan_count)
    weight = spectral.astype(jnp.float32).reshape(
        2, owned_row_modes, owned_col_modes, time_modes, chan_count, chan_count
    )
    weight_grad, back_modes = mix_modes(
        modes_in.reshape(mode_shape), modes_grad.reshape(mode_shape), weight, factor
    )
    grad_spectral = weight_grad.reshape(spectral.shape)
    flat_back = back_modes.reshape(owned_row_modes, 2, mode_width)
    mode_piece = lax.all_gather(flat_back, "row", axis=0, tiled=True)
    span_count = mode_piece.shape[0]
    frequencies = kept_freq(counting(span_count), row_modes)
    phases = phase_table(row_start + counting(row_count), frequencies, total_x, 1.0)
    rows_back = jnp.einsum("axpk,kpm->xam", phases, mode_piece, precision=exact_mode)
    rows_view = rows_back.reshape(row_count, 2, owned_col_modes, time_modes, chan_count)
    col_piece = lax.all_gather(rows_view.astype(jnp.bfloat16), "col", axis=2, tiled=True).astype(
        jnp.float32
    )
    span_count = col_piece.shape[2]
    phases = phase_table(col_start + counting(col_count), counting(span_count), total_y, 1.0)
    cells_y = jnp.zeros(
        (row_count, col_count, 2, time_modes, chan_count), jnp.float32
    ) + jnp.einsum("aypk,rpksc->ryasc", phases, col_piece, precision=exact_mode)
    kernel_grad = jnp.einsum(
        "ryasc,ast->rytc", cells_y, time_inverse(step_count, time_modes), precision=exact_mode
    )
    bypass_grad = jnp.einsum("nd,cd->nc", flat_grad, bypass, preferred_element_type=jnp.float32)
    total_grad = kernel_grad.reshape(-1, chan_count) + bypass_grad
    grad_inputs = total_grad.reshape(inputs.shape).astype(jnp.bfloat16)
    return (grad_inputs, grad_spectral, grad_bypass)


def solution(mesh):
    return jax.shard_map(
        local,
        mesh=mesh,
        in_specs=(
            P("row", "col", None),
            P("row", "col", None),
            P("row", "col", None),
            P(None, "row", "col", None, None),
            P(),
        ),
        out_specs=(P("row", "col", None), P(None, "row", "col", None, None), P()),
        check_vma=False,
    )
```

profile of v0, /device:TPU:1, one launch (start us, length us, event | category | flops | bytes accessed | tf_op | source)
XLA Modules:
  0.0 559.1 jit_solution(7331010780301432505)
XLA Ops:
  7.3 0.1 sine_multiply_fusion
  7.4 0.1 fusion.55
  7.6 1.1 copy.66
  8.7 1.1 copy.67
  9.8 0.3 fusion.22
  10.1 0.6 convolution_bitcast_fusion.2
  10.7 0.7 fusion.7
  11.4 0.6 copy.118
  12.0 0.7 reshape.836
  12.7 1.1 copy.62
  13.9 0.6 convolution_bitcast_fusion.3
  14.5 0.7 fusion.8
  15.2 0.6 copy.115
  15.8 0.7 reshape.835
  16.6 11.9 %convolution_bitcast_fusion = f32[128,2,2,10240]{0,3,1,2:T(8,128)} fusion(bf16[4,2,1,10240]{3,0,1,2:T(4,128)(2,1)S(1)} %reshape.836, bf16[4,2,1,10240]{3,0,1,2:T(4,128)(2,1)S(1)} %reshape.835, f32[1,128,2,4]{1,3,2,0:T(4,128)S(1)} %get-tuple-element.34, f32[1,128,2,4]{1,3,2,0:T(4,128)S(1)} %get-tuple-element.33), kind=kOutput, calls=%fused_computation.1 | convolution fusion | flops 503973888 | bytes 21307392 | tf_op jit(solution)/shard_map/akpr,rpbm->kabm/dot_general | solution.py:124
  28.5 31.0 %copy.73 = f32[128,2,2,10240]{3,2,1,0:T(2,128)} copy(f32[128,2,2,10240]{0,3,1,2:T(8,128)} %convolution_bitcast_fusion) | data formatting | bytes 41943040 | tf_op jit(solution)/shard_map/akpr,rpbm->kabm/transpose | solution.py:124
  59.5 0.6 all-gather.2.cloned.1.call-start
  60.1 4.9 fusion.97
  65.0 6.0 %copy.126 = bf16[1,4,64,5,1024]{2,4,3,1,0:T(8,128)(2,1)} copy(bf16[1,4,64,5,1024]{4,2,3,1,0:T(8,128)(2,1)} %get-tuple-element.18) | data formatting | bytes 5242880
  71.0 18.6 %copy.103 = bf16[4,64,5,32,32]{3,4,2,1,0:T(8,128)(2,1)} copy(bf16[4,64,5,32,32]{1,4,3,2,0:T(8,128)(2,1)} %bitcast.155) | data formatting | bytes 5242880 | tf_op jit(solution)/shard_map/squeeze | solution.py:62
  89.6 4.2 copy.125
  93.8 18.7 %copy.100 = bf16[4,64,5,32,32]{3,4,2,1,0:T(8,128)(2,1)} copy(bf16[4,64,5,32,32]{1,4,3,2,0:T(8,128)(2,1)} %bitcast.156) | data formatting | bytes 5242880 | tf_op jit(solution)/shard_map/squeeze | solution.py:61
  112.5 278.1 %all-reduce.3.cloned.1.call-done = f32[128,2,2,10240]{3,2,1,0:T(2,128)} async-done(((f32[128,2,2,10240]{3,2,1,0:T(2,128)}), f32[128,2,2,10240]{3,2,1,0:T(2,128)}) %all-reduce.3.cloned.1.call-update) | async-done | bytes 20971536
  390.6 4.0 dynamic-slice_reduce_fusion
  394.6 2.1 reshape_squeeze.6
  396.7 3.2 slice_bitcast_fusion.5
  399.9 11.1 %fusion.31 = f32[4,64,5,1,32]{4,3,2,1,0:T(1,128)S(1)} fusion(bf16[4,64,5,32,32]{3,4,2,1,0:T(8,128)(2,1)} %copy.103, f32[4,64,5,32,1]{3,2,1,0,4:T(8,128)S(1)} %get-tuple-element.23), kind=kOutput, calls=%fused_computation.60 | convolution fusion | flops 15728640 | bytes 2949120 | tf_op jit(solution)/shard_map/kyscd,kysd->kysc/dot_general | solution.py:65
  411.1 9.5 %fusion.29 = f32[4,64,5,1,32]{4,3,2,1,0:T(1,128)} fusion(bf16[4,64,5,32,32]{3,4,2,1,0:T(8,128)(2,1)S(1)} %bitcast.160, f32[4,64,5,32,1]{3,2,1,0,4:T(8,128)S(1)} %get-tuple-element.23), kind=kOutput, calls=%fused_computation.58 | convolution fusion | flops 15728640 | bytes 2949120 | tf_op jit(solution)/shard_map/kyscd,kysd->kysc/dot_general | solution.py:68
  420.5 8.6 %fusion.35 = f32[4,64,5,1,32]{4,3,2,1,0:T(1,128)S(1)} fusion(bf16[4,64,5,32,32]{3,4,2,1,0:T(8,128)(2,1)S(1)} %bitcast.160, f32[4,64,5,32,1]{3,2,1,0,4:T(8,128)S(1)} %get-tuple-element.22), kind=kOutput, calls=%fused_computation.64 | convolution fusion | flops 15728640 | bytes 2949120 | tf_op jit(solution)/shard_map/kyscd,kysd->kysc/dot_general | solution.py:64
  429.2 9.5 %fusion.33 = f32[4,64,5,1,32]{4,3,2,1,0:T(1,128)} fusion(bf16[4,64,5,32,32]{3,4,2,1,0:T(8,128)(2,1)S(1)} %bitcast.158, f32[4,64,5,32,1]{3,2,1,0,4:T(8,128)S(1)} %get-tuple-element.22), kind=kOutput, calls=%fused_computation.62 | convolution fusion | flops 15728640 | bytes 2949120 | tf_op jit(solution)/shard_map/kyscd,kysd->kysc/dot_general | solution.py:69
  438.7 0.2 fusion.10
  438.9 0.3 stack.120
  439.2 1.4 fusion.9
  440.6 0.3 stack.121
  441.0 1.0 copy.76
  442.0 0.9 copy.82
  442.8 1.7 reshape.810
  444.5 1.7 reshape.809
  446.2 0.4 convolution_bitcast_fusion.8
  446.6 41.1 %psum.7 = f32[32,32]{0,1:T(8,128)S(1)} all-reduce(f32[32,32]{0,1:T(8,128)S(1)} %convolution_bitcast_fusion.8), channel_id=1, replica_groups=mesh['row'=32,'col'=1] {'row','col'}, use_global_device_ids=true, to_apply=%region_1.2 | all-reduce | flops 1024 | bytes 8192 | tf_op jit(solution)/shard_map/psum | solution.py:100
  487.7 0.7 copy.90
  488.4 0.6 sine_negate_fusion.1
  489.1 0.1 fusion.54
  489.3 0.1 fusion.51
  489.4 0.6 maximum_bitcast_fusion.9
  490.1 1.4 copy.86
  491.5 1.0 copy.88
  492.5 1.7 reshape_squeeze.7
  494.2 1.5 slice_bitcast_fusion.1
  495.7 1.4 copy.85
  497.2 1.5 copy.87
  498.6 4.0 add_multiply_fusion
  502.6 7.3 %pad_maximum_fusion = f32[2,4,64,5,1024]{2,4,3,1,0:T(8,128)} fusion(f32[1,4,64,5,1024]{2,4,3,1,0:T(8,128)S(1)} %bitcast.154, f32[1,4,64,5,1024]{2,4,3,1,0:T(8,128)S(1)} %bitcast.153), kind=kLoop, calls=%fused_computation | loop fusion | flops 2621440 | bytes 20971520 | tf_op jit(solution)/shard_map/stack | solution.py:60
  509.9 15.8 %copy.89 = f32[2,4,64,5,1024]{4,2,3,1,0:T(8,128)} copy(f32[2,4,64,5,1024]{2,4,3,1,0:T(8,128)} %pad_maximum_fusion) | data formatting | bytes 20971520
  525.8 3.7 all-gather.2.cloned.1.call-done
  529.5 12.3 %fusion.1 = bf16[4,2,10240]{2,0,1:T(4,128)(2,1)S(1)} fusion(f32[128,2,10240]{2,1,0:T(2,128)} %all-gather.2.cloned.1.call-done, f32[1,4,2,128]{3,1,2,0:T(4,128)S(1)} %get-tuple-element.32, f32[1,4,2,128]{3,1,2,0:T(4,128)S(1)} %get-tuple-element.31), kind=kOutput, calls=%fused_computation.4 | convolution fusion | flops 251742208 | bytes 10657792 | tf_op jit(solution)/shard_map/axpk,kpm->xam/dot_general | solution.py:144
  541.8 0.7 reshape.837
  542.6 0.7 convolution_bitcast_fusion.4
  543.3 1.8 convolution_bitcast_fusion.7
  545.2 1.7 copy.81
  546.9 1.4 copy.83
  548.3 1.5 fusion.4
  549.8 0.5 copy.84
  550.3 1.4 convert_element_type.177
  (37 shorter events, 0.5 us)
Async XLA Ops:
  7.2 541.1 %copy-start = (bf16[32,32]{1,0:T(8,128)(2,1)S(1)}, bf16[32,32]{1,0:T(8,128)(2,1)}, u32[]{:S(2)}) copy-start(bf16[32,32]{1,0:T(8,128)(2,1)} %param.9) | copy-start | bytes 6148
  7.2 383.4 %all-reduce.3.cloned.1.call-start = ((), (), s32[]{:S(2)}) async-start(), calls=%async_computation.1 | async-start | bytes 41943040
  59.5 470.0 %all-gather.2.cloned.1.call-start = ((), (), s32[]{:S(2)}) async-start(), calls=%async_computation | async-start | bytes 10813440 | tf_op jit(solution)/shard_map/all_gather | solution.py:140
  394.6 16.4 %slice-start.3 = ((s8[10485760]{0:T(1024)(128)(4,1)}), s8[2097152]{0:T(1024)(128)(4,1)S(1)}, s32[]{:S(2)}) async-start(s8[10485760]{0:T(1024)(128)(4,1)} %bitcast.159), calls=%async_computation.5 | async-start | bytes 4194304
  396.7 14.3 %slice-start.4 = ((s8[10485760]{0:T(1024)(128)(4,1)}), s8[4194304]{0:T(1024)(128)(4,1)S(1)}, s32[]{:S(2)}) async-start(s8[10485760]{0:T(1024)(128)(4,1)} %bitcast.159), calls=%async_computation.6 | async-start | bytes 8388608
  399.9 11.1 %slice-start.5 = ((s8[10485760]{0:T(1024)(128)(4,1)}), s8[4194304]{0:T(1024)(128)(4,1)S(1)}, s32[]{:S(2)}) async-start(s8[10485760]{0:T(1024)(128)(4,1)} %bitcast.159), calls=%async_computation.7 | async-start | bytes 8388608
  411.0 18.1 %slice-start = ((s8[10485760]{0:T(1024)(128)(4,1)}), s8[4194304]{0:T(1024)(128)(4,1)S(1)}, s32[]{:S(2)}) async-start(s8[10485760]{0:T(1024)(128)(4,1)} %bitcast.157), calls=%async_computation.2 | async-start | bytes 8388608
  411.0 18.1 %slice-start.1 = ((s8[10485760]{0:T(1024)(128)(4,1)}), s8[4194304]{0:T(1024)(128)(4,1)S(1)}, s32[]{:S(2)}) async-start(s8[10485760]{0:T(1024)(128)(4,1)} %bitcast.157), calls=%async_computation.3 | async-start | bytes 8388608
  420.5 8.6 %slice-start.2 = ((s8[10485760]{0:T(1024)(128)(4,1)}), s8[2097152]{0:T(1024)(128)(4,1)S(1)}, s32[]{:S(2)}) async-start(s8[10485760]{0:T(1024)(128)(4,1)} %bitcast.157), calls=%async_computation.4 | async-start | bytes 4194304
  429.2 10.0 %copy-start.1 = (f32[4,64,5,1,32]{4,3,2,1,0:T(1,128)S(1)}, f32[4,64,5,1,32]{4,3,2,1,0:T(1,128)}, u32[]{:S(2)}) copy-start(f32[4,64,5,1,32]{4,3,2,1,0:T(1,128)} %fusion.29) | copy-start | bytes 491524
  529.5 13.1 %copy-start.2 = (f32[1,128,2,64]{1,3,2,0:T(8,128)S(1)}, f32[1,128,2,64]{1,3,2,0:T(8,128)}, u32[]{:S(2)}) copy-start(f32[1,128,2,64]{1,3,2,0:T(8,128)} %get-tuple-element.28) | copy-start | bytes 196612
  529.5 13.8 %copy-start.3 = (f32[1,5,8]{1,2,0:T(8,128)S(1)}, f32[1,5,8]{1,2,0:T(8,128)}, u32[]{:S(2)}) copy-start(f32[1,5,8]{1,2,0:T(8,128)} %get-tuple-element.47) | copy-start | bytes 484
  529.5 13.8 %copy-start.4 = (f32[1,5,8]{1,2,0:T(8,128)S(1)}, f32[1,5,8]{1,2,0:T(8,128)}, u32[]{:S(2)}) copy-start(f32[1,5,8]{1,2,0:T(8,128)} %get-tuple-element.48) | copy-start | bytes 484
Sparse Core Ops, SparseCore 0:
  59.6 330.9 all-reduce.2
  442.1 87.3 all-gather.1
where the time goes:
time: 568 us; the launch traced here: 559 us
  waiting for transfers between devices  282 us (50%)
  local copies, waits for them, and re-layouts  135 us (24%)
  matrix products  70 us (12%)
  blocking collectives  41.1 us (7%)
  other arithmetic  15.4 us (3%)
  between operations  14.9 us (3%)
    unnamed x3, waiting for transfers between devices  278 us
    psum x1, blocking collectives, local(): bypass_total = lax.psum(local_bypass, ('row', 'col'))  41.1 us
    transpose x1, local copies, waits for them, and re-layouts, local(): jnp.einsum('akpr,rpbm->kabm', phases, stacked, precision=exact_mode)  31 us
    unnamed x29, local copies, waits for them, and re-layouts  30.1 us
    squeeze x1, local copies, waits for them, and re-layouts, mix_modes(): w_real = weight[0]  18.7 us
    squeeze x1, local copies, waits for them, and re-layouts, mix_modes(): w_imag = weight[1]  18.6 us
    dot_general x1, matrix products, local(): jnp.einsum('axpk,kpm->xam', phases, mode_piece, precision=exact_mode)  12.3 us
    dot_general x1, matrix products, local(): jnp.einsum('akpr,rpbm->kabm', phases, stacked, precision=exact_mode)  11.9 us
  transfers between devices with their start and end apart: 2, of which 2 were waited for; matrix products, arithmetic and copies ran while one was open for 17% of the time, Pallas kernels for 0%

commit v1 on v0

--- a/solution.py
+++ b/solution.py
@@ -2,7 +2,10 @@
 
 import jax
 import jax.numpy as jnp
+import numpy as np
 from jax import lax
+from jax.experimental import pallas as pl
+from jax.experimental.pallas import tpu as pltpu
 from jax.sharding import PartitionSpec as P
 
 exact_mode = lax.Precision.HIGHEST
@@ -71,7 +74,7 @@
     return (weight_grad, jnp.stack([back_real, back_imag], axis=1))
 
 
-def local(inputs, preactivation, cotangent, spectral, bypass):
+def general_local(inputs, preactivation, cotangent, spectral, bypass):
     row_count, col_count, packed = inputs.shape
     chan_count = bypass.shape[0]
     step_count = packed // chan_count
@@ -160,6 +163,414 @@
     return (grad_inputs, grad_spectral, grad_bypass)
 
 
+BF = jnp.bfloat16
+LANES = 128
+SUB = 8
+
+
+def dot(a, b):
+    return jnp.dot(a, b, preferred_element_type=jnp.float32)
+
+
+def cos_sin(turns, length):
+    angles = 2.0 * np.pi * np.mod(turns, length) / length
+    return np.cos(angles), np.sin(angles)
+
+
+def build_tables(parts, rows, cols, steps, chans, row_modes, pair, kept, col_modes, time_modes):
+    lead = LANES // chans
+    eye = np.eye(chans)
+    t_index = np.arange(steps)
+    tables = {}
+    cos_t, sin_t = cos_sin(np.outer(t_index, np.arange(time_modes)), steps)
+    base = np.concatenate([np.kron(cos_t[:, :lead], eye), np.kron(-sin_t[:, :lead], eye)], axis=1)
+    last = np.kron(cos_t[:, lead:], eye)
+    blank = np.zeros_like(last)
+    tables["time_base"] = base
+    tables["time_last_in"] = np.concatenate(
+        [last, blank, blank, blank, blank, -last, blank, blank], axis=1
+    )
+    tables["time_last_grad"] = np.concatenate(
+        [blank, blank, last, blank, blank, blank, blank, -last], axis=1
+    )
+    ky = np.arange(col_modes)
+    y = np.arange(cols)
+    cos_y, sin_y = cos_sin(np.outer(ky, y), cols)
+    same_row = np.eye(rows)
+    tables["col_cos"] = np.einsum("ky,rs->krsy", cos_y, same_row).reshape(col_modes * rows, rows * cols)
+    tables["col_sin"] = np.einsum("ky,rs->krsy", sin_y, same_row).reshape(col_modes * rows, rows * cols)
+    slot = np.arange(row_modes)
+    freq = np.where(slot < row_modes // 2, slot, slot - row_modes)
+    total_x = parts * rows
+    cos_x, sin_x = cos_sin(np.outer(freq, np.arange(total_x)), total_x)
+    same_pair = np.eye(pair)
+
+    def spread(matrix):
+        blocks = matrix.reshape(parts, kept, parts, rows)
+        return np.einsum("ekdr,pq->epkdqr", blocks, same_pair).reshape(
+            parts * pair * kept, parts * pair * rows
+        )
+
+    tables["row_cos"] = spread(cos_x)
+    tables["row_sin"] = spread(sin_x)
+    tables["back_cos"] = spread(cos_x).T
+    tables["back_sin"] = spread(sin_x).T
+    swap = np.kron(np.array([[0.0, -1.0], [1.0, 0.0]]), eye)
+    tables["swap"] = np.kron(np.eye(LANES // (2 * chans)), swap)
+    order = np.zeros((kept, col_modes, parts, pair, kept))
+    for k in range(kept):
+        for e in range(parts):
+            for p in range(pair):
+                order[k, e * pair + p, e, p, k] = 1.0
+    tables["order"] = order.reshape(kept * col_modes, parts * pair * kept)
+    tables["unorder"] = tables["order"].T
+    wide = chans * chans
+    repeat = np.kron(eye, np.ones((1, chans)))
+    tiled = np.kron(np.ones((1, lead)), eye)
+    group = np.zeros((lead + 1, LANES, wide))
+    for k in range(lead):
+        group[k, k * chans : (k + 1) * chans] = repeat
+    extra = np.zeros((LANES, wide))
+    extra[chans : 2 * chans] = repeat
+    group[lead, :chans] = repeat
+    tables["repeat"] = np.concatenate([group, extra[None]], axis=0)
+    tiles = np.zeros((lead + 2, LANES, LANES))
+    for k in range(lead):
+        tiles[k, k * chans : (k + 1) * chans] = tiled
+    tiles[lead, 2 * chans : 3 * chans] = tiled
+    tiles[lead + 1, 3 * chans : 4 * chans] = tiled
+    tables["tile"] = tiles
+    tables["sums"] = np.tile(repeat.T, (1, lead))
+    re_c, re_s = np.kron(cos_t.T, eye), np.kron(sin_t.T, eye)
+    cut = lead * chans
+    rest = np.zeros((LANES - 2 * chans, steps * chans))
+    to_cos = np.concatenate([re_c[:cut], -re_s[:cut], re_c[cut:], -re_s[cut:], rest], axis=0)
+    to_sin = np.concatenate([-re_s[:cut], -re_c[:cut], -re_s[cut:], -re_c[cut:], rest], axis=0)
+    tables["time_back"] = np.concatenate([to_cos, to_sin], axis=1)
+    tables["col_back"] = np.concatenate([tables["col_cos"].T, tables["col_sin"].T], axis=1)
+    place = np.zeros((parts, SUB, chans))
+    for c in range(chans):
+        place[c, :, c] = 1.0
+    tables["place"] = place.reshape(parts * SUB, chans)
+    pick = np.zeros((parts, SUB))
+    pick[:, 0] = 1.0
+    tables["total"] = np.broadcast_to(pick.reshape(1, -1), (parts * SUB, parts * SUB))
+    first = np.zeros((chans, parts, SUB))
+    for c in range(chans):
+        first[c, c, 0] = 1.0
+    tables["first"] = first.reshape(chans, parts * SUB)
+    tables["spread_chan"] = np.kron(np.ones((steps, 1)), eye)
+    return {name: np.asarray(table, np.float32).astype(jnp.bfloat16) for name, table in tables.items()}
+
+
+def call(kernel, out_shapes, *operands, scratch=(), far=(), limit=12, keep=True):
+    near = pl.BlockSpec(memory_space=pltpu.VMEM)
+    stay = pl.BlockSpec(memory_space=pltpu.HBM)
+    space = lambda i: pltpu.HBM if i in far else pltpu.VMEM
+    operands = [pltpu.with_memory_space_constraint(a, space(i)) for i, a in enumerate(operands)]
+    hold = lambda a: pltpu.VMEM(a.shape, a.dtype) if keep else a
+    return pl.pallas_call(
+        kernel,
+        out_shape=jax.tree.map(hold, out_shapes),
+        in_specs=[stay if i in far else near for i in range(len(operands))],
+        out_specs=jax.tree.map(lambda _: near, out_shapes),
+        scratch_shapes=list(scratch),
+        compiler_params=pltpu.CompilerParams(vmem_limit_bytes=limit * 1024 * 1024),
+    )(*operands)
+
+
+def lane_blocks(values):
+    return [values[:, i * LANES : (i + 1) * LANES] for i in range(values.shape[1] // LANES)]
+
+
+def pack(blocks):
+    parts = blocks[0].shape[0] // SUB
+    stacked = jnp.concatenate([b.reshape(parts, SUB, LANES) for b in blocks], axis=1)
+    return stacked.reshape(-1, LANES).astype(BF)
+
+
+def unpack(rows, count):
+    cube = rows.astype(jnp.float32).reshape(-1, count * SUB, LANES)
+    return [cube[:, i * SUB : (i + 1) * SUB].reshape(-1, LANES).astype(BF) for i in range(count)]
+
+
+def lane_group(shape, chans):
+    return lax.broadcasted_iota(jnp.int32, shape, 1) // chans
+
+
+def halves(values, chans):
+    high = values.astype(BF).astype(jnp.float32)
+    group = lane_group(values.shape, chans)
+    return jnp.where(group == 2, high, jnp.where(group == 3, values - high, 0.0))
+
+
+def diagonal(values, chans):
+    row_step = lax.broadcasted_iota(jnp.int32, values.shape, 0) // chans
+    return jnp.where(row_step == lane_group(values.shape, chans), values, 0.0)
+
+
+def start_copies(sems, *pairs):
+    copies = [pltpu.make_async_copy(src, dst, sems.at[i]) for i, (src, dst) in enumerate(pairs)]
+    for copy in copies:
+        copy.start()
+    return copies
+
+
+def columns_kernel(
+    in_hbm, pre_hbm, cot_hbm, time_hbm, col_hbm, square_hbm, swap_hbm, tile_hbm, sums_hbm,
+    out_ref, grad_ref, square_ref, swap_ref, tile_ref, sums_ref,
+    in_ref, pre_ref, cot_ref, time_ref, col_ref, sems,
+):
+    copies = start_copies(
+        sems,
+        (pre_hbm, pre_ref), (cot_hbm, cot_ref), (in_hbm, in_ref), (time_hbm, time_ref), (col_hbm, col_ref),
+        (square_hbm, square_ref), (swap_hbm, swap_ref), (tile_hbm, tile_ref), (sums_hbm, sums_ref),
+    )
+    rows, cols, width = in_ref.shape
+    copies[0].wait()
+    slopes = gelu_slope(pre_ref[...].reshape(rows * cols, width).astype(jnp.float32))
+    copies[1].wait()
+    grad = (cot_ref[...].reshape(rows * cols, width).astype(jnp.float32) * slopes).astype(BF)
+    grad_ref[...] = grad
+    copies[2].wait()
+    copies[3].wait()
+    field = in_ref[...].reshape(rows * cols, width)
+    base, last_in, last_grad = [time_ref[i * width : (i + 1) * width] for i in range(3)]
+    time_in = dot(field, base)
+    time_grad = dot(grad, base)
+    last = dot(field, last_in) + dot(grad, last_grad)
+    in_re, in_im = time_in[:, :LANES], time_in[:, LANES:]
+    gr_re, gr_im = time_grad[:, :LANES], time_grad[:, LANES:]
+    direct = jnp.concatenate([in_re, in_im, gr_re, gr_im, last[:, :LANES]], axis=1).astype(BF)
+    turned = jnp.concatenate([in_im, -in_re, gr_im, -gr_re, last[:, LANES:]], axis=1).astype(BF)
+    copies[4].wait()
+    half = col_ref.shape[0] // 2
+    modes = dot(col_ref[:half], direct) + dot(col_ref[half:], turned)
+    out_ref[...] = pack(lane_blocks(modes))
+    for copy in copies[5:]:
+        copy.wait()
+
+
+def bypass_terms(field, grad, place, chans):
+    products = lax.dot_general(
+        field, grad, (((0,), (0,)), ((), ())), preferred_element_type=jnp.float32
+    )
+    products = diagonal(products, chans)
+    partial = products[:chans]
+    for step in range(1, field.shape[1] // chans):
+        partial = partial + products[step * chans : (step + 1) * chans]
+    folded = sum(lane_blocks(partial))
+    shift = LANES // 2
+    while shift >= chans:
+        folded = folded + pltpu.roll(folded, shift, 1)
+        shift //= 2
+    return dot(place, halves(folded, chans).astype(BF))
+
+
+def mixing_kernel(sent_hbm, grad_hbm, long_hbm, bypass_ref, spread_ref, mixed_ref, long_ref, grad_ref, sems):
+    del sent_hbm
+    copies = start_copies(sems, (grad_hbm, grad_ref), (long_hbm, long_ref))
+    chans = bypass_ref.shape[0]
+    spread = spread_ref[...]
+    across = lax.dot_general(
+        bypass_ref[...], spread, (((0,), (1,)), ((), ())), preferred_element_type=jnp.float32
+    ).astype(BF)
+    matrix = diagonal(dot(spread, across), chans).astype(BF)
+    copies[0].wait()
+    mixed_ref[...] = dot(grad_ref[...], matrix)
+    copies[1].wait()
+
+
+def rows_kernel(in_ref, square_ref, swap_ref, out_ref):
+    in_re, in_im, gr_re, gr_im, last = unpack(in_ref[...], 5)
+    size = square_ref.shape[1]
+    turned_last = dot(last, swap_ref[...]).astype(BF)
+    direct = jnp.concatenate([in_re, in_im, gr_re, gr_im, last], axis=1)
+    turned = jnp.concatenate([in_im, -in_re, gr_im, -gr_re, turned_last], axis=1)
+    modes = dot(square_ref[:size], direct) + dot(square_ref[size : 2 * size], turned)
+    out_ref[...] = pack(lane_blocks(modes))
+
+
+def back_kernel(
+    in_ref, grad_ref, weight_ref, field_ref, square_ref, tile_ref, sums_ref, place_ref, out_ref, modes_ref,
+    *, factor,
+):
+    chans = place_ref.shape[1]
+    size = square_ref.shape[1]
+    lanes = jnp.concatenate(unpack(in_ref[...], 5), axis=1)
+    modes = dot(square_ref[4 * size : 5 * size], lanes).astype(BF)
+    modes_ref[...] = modes
+    rows, cols, width = field_ref.shape
+    terms = bypass_terms(field_ref[...].reshape(rows * cols, width), grad_ref[...], place_ref[...], chans)
+    steps = weight_ref.shape[2]
+    wide = weight_ref.shape[4]
+    lead = LANES // chans
+    gr_re, gr_im, last = lane_blocks(modes)[2:]
+    first = jnp.concatenate([gr_re, gr_im], axis=0)
+    group = lane_group((size, LANES), chans)
+    re_sum = im_sum = jnp.zeros((size, LANES), jnp.float32)
+    for k in range(steps):
+        if k < lead:
+            g_both = dot(first, tile_ref[k]).astype(BF)
+            g_re, g_im = g_both[:size], g_both[size:]
+        else:
+            g_re, g_im = dot(last, tile_ref[lead]).astype(BF), dot(last, tile_ref[lead + 1]).astype(BF)
+        p_re, p_im = [], []
+        for j in range(wide // LANES):
+            w_re = weight_ref[0, :, k, :, j * LANES : (j + 1) * LANES].reshape(size, LANES)
+            w_im = weight_ref[1, :, k, :, j * LANES : (j + 1) * LANES].reshape(size, LANES)
+            p_re.append(w_re * g_re + w_im * g_im)
+            p_im.append(w_re * g_im - w_im * g_re)
+        both = jnp.concatenate([jnp.concatenate(p_re, axis=1), jnp.concatenate(p_im, axis=1)], axis=0)
+        summed = dot(both, sums_ref[...])
+        if k < lead:
+            re_sum = jnp.where(group == k, summed[:size], re_sum)
+            im_sum = jnp.where(group == k, summed[size:], im_sum)
+        else:
+            last_sum = jnp.where(group == 0, summed[:size], jnp.where(group == 1, summed[size:], 0.0))
+    back = (jnp.concatenate([re_sum, im_sum, last_sum], axis=1) * factor).astype(BF)
+    re, im, last = lane_blocks(dot(square_ref[5 * size : 6 * size], back))
+    out_ref[...] = pack([re, im, last + terms])
+
+
+def weight_kernel(modes_ref, repeat_ref, tile_ref, out_ref, *, factor):
+    modes = modes_ref[...]
+    in_re, in_im, gr_re, gr_im, last = [modes[:, i * LANES : (i + 1) * LANES] for i in range(5)]
+    steps = out_ref.shape[2]
+    lead = tile_ref.shape[0] - 2
+    wide = out_ref.shape[-1]
+    for k in range(steps):
+        if k < lead:
+            a_re, a_im = dot(in_re, repeat_ref[k]), dot(in_im, repeat_ref[k])
+            b_re, b_im = dot(gr_re, tile_ref[k]), dot(gr_im, tile_ref[k])
+        else:
+            a_re, a_im = dot(last, repeat_ref[lead]), dot(last, repeat_ref[lead + 1])
+            b_re, b_im = dot(last, tile_ref[lead]), dot(last, tile_ref[lead + 1])
+        b_re = jnp.concatenate([b_re * factor] * (wide // LANES), axis=1)
+        b_im = jnp.concatenate([b_im * factor] * (wide // LANES), axis=1)
+        out_ref[0, 0, k] = a_re * b_re + a_im * b_im
+        out_ref[1, 0, k] = a_re * b_im - a_im * b_re
+
+
+def rows_back_kernel(in_ref, square_ref, swap_ref, out_ref, *, chans):
+    re, im, tail = unpack(in_ref[...], 3)
+    size = square_ref.shape[1]
+    group = lane_group(tail.shape, chans)
+    last = jnp.where(group < 2, tail.astype(jnp.float32), 0.0).astype(BF)
+    turned_last = dot(-last, swap_ref[...]).astype(BF)
+    direct = jnp.concatenate([re, im, last], axis=1)
+    turned = jnp.concatenate([-im, re, turned_last], axis=1)
+    rows = dot(square_ref[2 * size : 3 * size], direct) + dot(square_ref[3 * size : 4 * size], turned)
+    summed = dot(square_ref[6 * size : 7 * size], tail)
+    summed = summed + pltpu.roll(summed, LANES - chans, 1)
+    summed = jnp.where(group == 2, summed, 0.0)
+    summed = summed + pltpu.roll(summed, chans, 1)
+    re, im, last = lane_blocks(rows)
+    out_ref[...] = pack([re, im, last + halves(summed, chans)])
+
+
+def columns_back_kernel(in_ref, mixed_ref, square_ref, long_ref, out_ref, bypass_ref, *, factor):
+    rows, cols, width = out_ref.shape
+    chans = bypass_ref.shape[0]
+    size = square_ref.shape[1]
+    blocks = unpack(in_ref[...], 3)
+    lanes = jnp.concatenate(blocks, axis=1)
+    height = lanes.shape[1]
+    steps = dot(lanes, long_ref[:height]).astype(BF)
+    stacked = jnp.concatenate([steps[:, :width], steps[:, width:]], axis=0)
+    total = dot(long_ref[height:], stacked) + mixed_ref[...]
+    out_ref[...] = total.reshape(rows, cols, width).astype(BF)
+    sums = dot(square_ref[7 * size :], blocks[2])
+    sums = pltpu.roll(sums + pltpu.roll(sums, LANES - chans, 1), LANES // 2, 1)
+    bypass_ref[...] = sums[:, :chans] * factor
+
+
+def local(inputs, preactivation, cotangent, spectral, bypass):
+    rows, cols, width = inputs.shape
+    chans = bypass.shape[0]
+    steps = width // chans
+    kept, col_modes, time_modes, wide = spectral.shape[1:]
+    parts = lax.axis_size("row")
+    pair = col_modes // parts
+    fits = (
+        lax.axis_size("col") == 1
+        and col_modes % parts == 0
+        and pair * rows == SUB
+        and pair * kept == SUB
+        and parts == chans
+        and 4 * chans == LANES
+        and time_modes == 5
+        and steps == 8
+        and cols % LANES == 0
+    )
+    if not fits:
+        return general_local(inputs, preactivation, cotangent, spectral, bypass)
+    row_modes = kept * parts
+    total_x = rows * parts
+    factor = 1.0 / math.sqrt(float(total_x * cols * steps * row_modes * col_modes * time_modes))
+    bypass_factor = 1.0 / math.sqrt(float(total_x * cols * steps))
+    tables = build_tables(parts, rows, cols, steps, chans, row_modes, pair, kept, col_modes, time_modes)
+    stack = lambda *names: jnp.asarray(np.concatenate([tables[name] for name in names], axis=0))
+    time_table = stack("time_base", "time_last_in", "time_last_grad")
+    col_table = stack("col_cos", "col_sin")
+    square = stack("row_cos", "row_sin", "back_cos", "back_sin", "order", "unorder", "total", "first")
+    long = stack("time_back", "col_back")
+    swap, tile, repeat, sums, spread, place = [
+        jnp.asarray(tables[name]) for name in ("swap", "tile", "repeat", "sums", "spread_chan", "place")
+    ]
+
+    def swap_parts(array):
+        return lax.all_to_all(array, "row", 0, 0, tiled=True)
+
+    like = lambda array: jax.ShapeDtypeStruct(array.shape, array.dtype)
+    shape = jax.ShapeDtypeStruct
+    chunk = parts * SUB
+    field = (rows * cols, width)
+    sent, pre_grad, square, swap, tile, sums = call(
+        columns_kernel,
+        (shape((5 * chunk, LANES), BF), shape(field, BF)) + tuple(like(a) for a in (square, swap, tile, sums)),
+        inputs, preactivation, cotangent, time_table, col_table, square, swap, tile, sums,
+        far=range(9),
+        scratch=[pltpu.VMEM(a.shape, a.dtype) for a in (inputs, inputs, inputs, time_table, col_table)]
+        + [pltpu.SemaphoreType.DMA((9,))],
+    )
+    sent = call(rows_kernel, shape((5 * chunk, LANES), BF), swap_parts(sent), square, swap)
+    weight = spectral.transpose(0, 1, 3, 2, 4)
+    sent, modes = call(
+        lambda *refs: back_kernel(*refs, factor=factor),
+        (shape((3 * chunk, LANES), BF), shape((kept * col_modes, 5 * LANES), BF)),
+        swap_parts(sent), pre_grad, weight, inputs, square, tile, sums, place,
+    )
+    whole = lambda a: pl.BlockSpec(a.shape, lambda i: (0,) * a.ndim)
+    grad_spectral = pl.pallas_call(
+        lambda *refs: weight_kernel(*refs, factor=factor),
+        grid=(kept,),
+        out_shape=shape((2, kept, time_modes, col_modes, wide), jnp.float32),
+        in_specs=[pl.BlockSpec((col_modes, 5 * LANES), lambda i: (i, 0)), whole(repeat), whole(tile)],
+        out_specs=pl.BlockSpec((2, 1, time_modes, col_modes, wide), lambda i: (0, i, 0, 0, 0)),
+        compiler_params=pltpu.CompilerParams(vmem_limit_bytes=16 * 1024 * 1024),
+    )(modes, repeat, tile).transpose(0, 1, 3, 2, 4)
+    sent = call(
+        lambda *refs: rows_back_kernel(*refs, chans=chans),
+        shape((3 * chunk, LANES), BF),
+        swap_parts(sent), square, swap,
+    )
+    mixed, long = call(
+        mixing_kernel,
+        (shape(field, jnp.float32), like(long)),
+        sent, pre_grad, long, bypass, spread,
+        far=(0, 1, 2),
+        scratch=[pltpu.VMEM(field, BF), pltpu.SemaphoreType.DMA((2,))],
+    )
+    grad_inputs, grad_bypass = call(
+        lambda *refs: columns_back_kernel(*refs, factor=bypass_factor),
+        (shape((rows, cols, width), BF), shape((chans, chans), jnp.float32)),
+        swap_parts(sent), mixed, square, long,
+        keep=False,
+    )
+    return (grad_inputs, grad_spectral, grad_bypass)
+
+
 def solution(mesh):
     return jax.shard_map(
         local,

time: 568 us -> 66.1 us (0.12); the launches traced: 559 us -> 65.8 us
  waiting for transfers between devices: 282 us -> 2.24 us
  local copies, waits for them, and re-layouts: 135 us -> 0.04 us
  matrix products: 70 us -> 0 us
  Pallas kernels: 0 us -> 15.9 us
  other arithmetic: 15.4 us -> 0 us
  between operations: 14.9 us -> 0.75 us
    unnamed x3 -> x0, waiting for transfers between devices: 278 us -> none
    dot_general x14 -> x0, matrix products: 70 us -> none  [the longest x1 12.3 us: local(): jnp.einsum('axpk,kpm->xam', phases, mode_piece, precision=exact_mode)]
    all_to_all x0 -> x3, blocking collectives: none -> 44.6 us  [swap_parts(): return lax.all_to_all(array, 'row', 0, 0, tiled=True)]
    squeeze x5 -> x0, local copies, waits for them, and re-layouts: 42.9 us -> none  [the longest x1 18.7 us: mix_modes(): w_real = weight[0]]
    psum x1 -> x0, blocking collectives: 41.1 us -> none  [local(): bypass_total = lax.psum(local_bypass, ('row', 'col'))]
    transpose x2 -> x0, local copies, waits for them, and re-layouts: 32.7 us -> none  [the longest x1 31 us: local(): jnp.einsum('akpr,rpbm->kabm', phases, stacked, precision=exact_mode)]
    unnamed x29 -> x14, local copies, waits for them, and re-layouts: 30.1 us -> 0.04 us
    pallas_call x0 -> x7, Pallas kernels: none -> 15.9 us  [the longest x6 10.2 us: call(): pl.pallas_call(kernel, out_shape=jax.tree.map(hold, out_shapes), in_specs...]
  transfers between devices with their start and end apart: 2 -> 1, of which waited for: 2 -> 1; matrix products, arithmetic and copies ran while one was open for 17% -> 0% of each run, Pallas kernels for 0% -> 11%
where the time goes in v1:
time: 66.1 us; the launch traced here: 65.8 us
  blocking collectives  44.6 us (67%)
  Pallas kernels  15.9 us (24%)
  starting transfers between devices  2.37 us (4%)
  waiting for transfers between devices  2.24 us (3%)
  between operations  0.75 us (1%)
    all_to_all x3, blocking collectives, swap_parts(): return lax.all_to_all(array, 'row', 0, 0, tiled=True)  44.6 us
    pallas_call x6, Pallas kernels, call(): pl.pallas_call(kernel, out_shape=jax.tree.map(hold, out_shapes), in_specs...  10.2 us
    pallas_call x1, Pallas kernels, local(): pl.pallas_call(lambda *refs: weight_kernel(*refs, factor=factor), grid=(k...  5.65 us
    all_to_all x1, starting transfers between devices, swap_parts(): return lax.all_to_all(array, 'row', 0, 0, tiled=True)  2.37 us
    all_to_all x1, waiting for transfers between devices, swap_parts(): return lax.all_to_all(array, 'row', 0, 0, tiled=True)  2.24 us
  transfers between devices with their start and end apart: 1, of which 1 were waited for; matrix products, arithmetic and copies ran while one was open for 0% of the time, Pallas kernels for 11%

profile of v1, /device:TPU:1, one launch (start us, length us, event | category | flops | bytes accessed | tf_op | source)
XLA Modules:
  0.0 65.8 jit_solution(5666707870133050507)
XLA Ops:
  0.6 0.0 copy-start.4
  0.6 0.0 copy-start.2
  0.7 0.0 copy-start
  0.7 3.0 %shard_map.166 = (bf16[1280,128]{1,0:T(8,128)(2,1)S(1)}, bf16[512,256]{1,0:T(8,128)(2,1)S(1)}, bf16[1824,256]{1,0:T(8,128)(2,1)S(1)}, bf16[128,128]{1,0:T(8,128)...) custom-call(bf16[4,128,256]{2,1,0:T(8,128)(2,1)} %refs_3_.1, bf16[4,128,256]{2,1,0:T(8,128)(2,1)} %pre_hbm.1, ...), custom_call_target="tpu_custom_call" | custom-call | tf_op jit(solution)/shard_map/pallas_call | solution.py:272
  3.6 0.0 copy-start.3
  3.6 18.2 %all_to_all.44 = bf16[32,40,128]{2,1,0:T(8,128)(2,1)S(1)} all-to-all(bf16[32,40,128]{2,1,0:T(8,128)(2,1)S(1)} %bitcast.16), channel_id=1, replica_groups=mesh['row'=32,'col'=1] {'row'}, dimensions={0} | all-to-all | bytes 655360 | tf_op jit(solution)/shard_map/all_to_all | solution.py:523
  21.8 0.4 shard_map.167
  22.3 0.0 copy-start.1
  22.3 14.2 %all_to_all.45 = bf16[32,40,128]{2,1,0:T(8,128)(2,1)S(1)} all-to-all(bf16[32,40,128]{2,1,0:T(8,128)(2,1)S(1)} %bitcast.13), channel_id=1, replica_groups=mesh['row'=32,'col'=1] {'row'}, dimensions={0} | all-to-all | bytes 655360 | tf_op jit(solution)/shard_map/all_to_all | solution.py:523
  36.5 0.0 copy-done.4
  36.5 0.0 copy-done.2
  36.5 0.0 copy-done
  36.5 3.1 %shard_map.168 = (bf16[768,128]{1,0:T(8,128)(2,1)S(1)}, bf16[256,640]{1,0:T(8,128)(2,1)S(1)}) custom-call(bf16[1280,128]{1,0:T(8,128)(2,1)S(1)} %bitcast.11, bf16[512,256]{1,0:T(8,128)(2,1)S(1)} %get-tuple-element.18.refs_1_.grad_hbm, bf16[2,4,5,64,1024]{4,3,2,1,0:T(8,128)(2,1)S(1)} %bitcast.10, bf16[4,128,256]{2,1,0:T(8,128)(2,1)S(1)} %copy-done.2, ...), custom_call_target="tpu_custom_call" | custom-call | tf_op jit(solution)/shard_map/pallas_call | solution.py:272
  39.6 0.0 copy-done.3
  39.6 12.2 %all_to_all.46 = bf16[32,24,128]{2,1,0:T(8,128)(2,1)S(1)} all-to-all(bf16[32,24,128]{2,1,0:T(8,128)(2,1)S(1)} %bitcast.17), channel_id=1, replica_groups=mesh['row'=32,'col'=1] {'row'}, dimensions={0} | all-to-all | bytes 393216 | tf_op jit(solution)/shard_map/all_to_all | solution.py:523
  51.7 1.2 %shard_map.169.sent_hbm = bf16[768,128]{1,0:T(8,128)(2,1)} custom-call(bf16[768,128]{1,0:T(8,128)(2,1)S(1)} %bitcast.15, bf16[1824,256]{1,0:T(8,128)(2,1)S(1)} %get-tuple-element.16.square_ref.refs_4_.refs_1_.refs_2_, bf16[128,128]{1,0:T(8,128)(2,1)S(1)} %get-tuple-element.17.swap_ref.refs_2_), custom_call_target="tpu_custom_call" | custom-call | tf_op jit(solution)/shard_map/pallas_call | solution.py:272
  52.9 2.4 %all-to-all-start.3 = ((bf16[32,24,128]{2,1,0:T(8,128)(2,1)}), bf16[32,24,128]{2,1,0:T(8,128)(2,1)S(1)}, u32[]{:S(2)}, u32[]{:S(2)}) async-start(bf16[32,24,128]{2,1,0:T(8,128)(2,1)} %bitcast.7), calls=%async_computation.3 | async-start | bytes 393216 | tf_op jit(solution)/shard_map/all_to_all | solution.py:523
  55.3 0.0 copy-done.1
  55.3 0.0 copy-start.5
  55.3 0.0 copy-start.6
  55.3 5.7 %shard_map.172 = f32[2,4,5,64,1024]{4,3,2,1,0:T(8,128)} custom-call(bf16[256,640]{1,0:T(8,128)(2,1)S(1)} %get-tuple-element.25.refs_0_, bf16[6,128,1024]{2,1,0:T(8,128)(2,1)S(1)} %copy-done.1, bf16[6,128,128]{2,1,0:T(8,128)(2,1)S(1)} %get-tuple-element.19.refs_5_.refs_2_), custom_call_target="tpu_custom_call" | custom-call | tf_op jit(solution)/shard_map/pallas_call | solution.py:545
  61.0 0.0 copy-done.5
  61.0 0.0 copy-done.6
  61.0 1.3 %shard_map.170 = (f32[512,256]{1,0:T(8,128)S(1)}, bf16[896,512]{1,0:T(8,128)(2,1)S(1)}) custom-call(bf16[768,128]{1,0:T(8,128)(2,1)} %shard_map.169.sent_hbm, bf16[512,256]{1,0:T(8,128)(2,1)} %copy-done.3, bf16[896,512]{1,0:T(8,128)(2,1)} %constant.23.clone.long_hbm, bf16[32,32]{1,0:T(8,128)(2,1)S(1)} %copy-done.6, bf16[256,32]{1,0:T(8,128)(2,1)S(1)} %copy-done.5), custom_call_target="tpu_custom_call" | custom-call | tf_op jit(solution)/shard_map/pallas_call | solution.py:272
  62.3 2.2 %all-to-all-done.3 = bf16[32,24,128]{2,1,0:T(8,128)(2,1)S(1)} async-done(((bf16[32,24,128]{2,1,0:T(8,128)(2,1)}), bf16[32,24,128]{2,1,0:T(8,128)(2,1)S(1)}, u32[]{:S(2)}, u32[]{:S(2)}) %all-to-all-start.3) | async-done | bytes 196640 | tf_op jit(solution)/shard_map/all_to_all | solution.py:523
  64.5 1.3 %shard_map.171 = (bf16[4,128,256]{2,1,0:T(8,128)(2,1)}, f32[32,32]{1,0:T(8,128)}) custom-call(bf16[768,128]{1,0:T(8,128)(2,1)S(1)} %bitcast.14, f32[512,256]{1,0:T(8,128)S(1)} %get-tuple-element.22.refs_1_, bf16[1824,256]{1,0:T(8,128)(2,1)S(1)} %get-tuple-element.16.square_ref.refs_4_.refs_1_.refs_2_, bf16[896,512]{1,0:T(8,128)(2,1)S(1)} %get-tuple-element.23.refs_3_), custom_call_target="tpu_custom_call" | custom-call | tf_op jit(solution)/shard_map/pallas_call | solution.py:272
Async XLA Ops:
  0.6 35.9 %copy-start.4 = (bf16[256,32]{1,0:T(8,128)(2,1)S(1)}, bf16[256,32]{1,0:T(8,128)(2,1)}, u32[]{:S(2)}) copy-start(bf16[256,32]{1,0:T(8,128)(2,1)} %constant.29.clone.refs_7_) | copy-start | bytes 49156
  0.6 35.9 %copy-start.2 = (bf16[4,128,256]{2,1,0:T(8,128)(2,1)S(1)}, bf16[4,128,256]{2,1,0:T(8,128)(2,1)}, u32[]{:S(2)}) copy-start(bf16[4,128,256]{2,1,0:T(8,128)(2,1)} %refs_3_.1) | copy-start | bytes 786436
  0.7 35.9 %copy-start = (bf16[2,4,64,5,1024]{4,2,3,1,0:T(8,128)(2,1)S(1)}, bf16[2,4,64,5,1024]{4,2,3,1,0:T(8,128)(2,1)}, u32[]{:S(2)}) copy-start(bf16[2,4,64,5,1024]{4,2,3,1,0:T(8,128)(2,1)} %param.18) | copy-start | bytes 15728644
  3.6 36.0 %copy-start.3 = (bf16[512,256]{1,0:T(8,128)(2,1)}, bf16[512,256]{1,0:T(8,128)(2,1)S(1)}, u32[]{:S(2)}) copy-start(bf16[512,256]{1,0:T(8,128)(2,1)S(1)} %get-tuple-element.18.refs_1_.grad_hbm) | copy-start | bytes 786436
  22.3 33.0 %copy-start.1 = (bf16[6,128,1024]{2,1,0:T(8,128)(2,1)S(1)}, bf16[6,128,1024]{2,1,0:T(8,128)(2,1)}, u32[]{:S(2)}) copy-start(bf16[6,128,1024]{2,1,0:T(8,128)(2,1)} %constant.26.clone.refs_1_) | copy-start | bytes 4718596
  52.9 11.6 %all-to-all-start.3 = ((bf16[32,24,128]{2,1,0:T(8,128)(2,1)}), bf16[32,24,128]{2,1,0:T(8,128)(2,1)S(1)}, u32[]{:S(2)}, u32[]{:S(2)}) async-start(bf16[32,24,128]{2,1,0:T(8,128)(2,1)} %bitcast.7), calls=%async_computation.3 | async-start | bytes 393216 | tf_op jit(solution)/shard_map/all_to_all | solution.py:523
  55.3 5.7 %copy-start.5 = (bf16[256,32]{1,0:T(8,128)(2,1)S(1)}, bf16[256,32]{1,0:T(8,128)(2,1)}, u32[]{:S(2)}) copy-start(bf16[256,32]{1,0:T(8,128)(2,1)} %constant.28.clone.spread_ref) | copy-start | bytes 49156
  55.3 5.7 %copy-start.6 = (bf16[32,32]{1,0:T(8,128)(2,1)S(1)}, bf16[32,32]{1,0:T(8,128)(2,1)}, u32[]{:S(2)}) copy-start(bf16[32,32]{1,0:T(8,128)(2,1)} %bypass_ref.1) | copy-start | bytes 6148

commit v2 on v1

--- a/solution.py
+++ b/solution.py
@@ -183,22 +183,16 @@
     t_index = np.arange(steps)
     tables = {}
     cos_t, sin_t = cos_sin(np.outer(t_index, np.arange(time_modes)), steps)
-    base = np.concatenate([np.kron(cos_t[:, :lead], eye), np.kron(-sin_t[:, :lead], eye)], axis=1)
-    last = np.kron(cos_t[:, lead:], eye)
-    blank = np.zeros_like(last)
-    tables["time_base"] = base
-    tables["time_last_in"] = np.concatenate(
-        [last, blank, blank, blank, blank, -last, blank, blank], axis=1
-    )
-    tables["time_last_grad"] = np.concatenate(
-        [blank, blank, last, blank, blank, blank, blank, -last], axis=1
-    )
+    real = [np.kron(cos_t[:, k : k + 1], eye) for k in range(time_modes)]
+    imag = [np.kron(-sin_t[:, k : k + 1], eye) for k in range(1, lead)]
+    tables["time"] = np.concatenate(real + imag, axis=1)
     ky = np.arange(col_modes)
     y = np.arange(cols)
     cos_y, sin_y = cos_sin(np.outer(ky, y), cols)
+    tables["col"] = np.repeat(np.concatenate([cos_y, sin_y], axis=0), rows, axis=0)
     same_row = np.eye(rows)
-    tables["col_cos"] = np.einsum("ky,rs->krsy", cos_y, same_row).reshape(col_modes * rows, rows * cols)
-    tables["col_sin"] = np.einsum("ky,rs->krsy", sin_y, same_row).reshape(col_modes * rows, rows * cols)
+    col_cos = np.einsum("ky,rs->krsy", cos_y, same_row).reshape(col_modes * rows, rows * cols)
+    col_sin = np.einsum("ky,rs->krsy", sin_y, same_row).reshape(col_modes * rows, rows * cols)
     slot = np.arange(row_modes)
     freq = np.where(slot < row_modes // 2, slot, slot - row_modes)
     total_x = parts * rows
@@ -234,12 +228,9 @@
     extra[chans : 2 * chans] = repeat
     group[lead, :chans] = repeat
     tables["repeat"] = np.concatenate([group, extra[None]], axis=0)
-    tiles = np.zeros((lead + 2, LANES, LANES))
-    for k in range(lead):
-        tiles[k, k * chans : (k + 1) * chans] = tiled
-    tiles[lead, 2 * chans : 3 * chans] = tiled
-    tiles[lead + 1, 3 * chans : 4 * chans] = tiled
-    tables["tile"] = tiles
+    spots = np.eye(lead)
+    tables["tile"] = np.concatenate([np.kron(spots[:, k : k + 1], tiled) for k in range(lead)], axis=1)
+    tables["tile_last"] = np.concatenate([np.kron(spots[:, k : k + 1], tiled) for k in (2, 3)], axis=1)
     tables["sums"] = np.tile(repeat.T, (1, lead))
     re_c, re_s = np.kron(cos_t.T, eye), np.kron(sin_t.T, eye)
     cut = lead * chans
@@ -247,7 +238,7 @@
     to_cos = np.concatenate([re_c[:cut], -re_s[:cut], re_c[cut:], -re_s[cut:], rest], axis=0)
     to_sin = np.concatenate([-re_s[:cut], -re_c[:cut], -re_s[cut:], -re_c[cut:], rest], axis=0)
     tables["time_back"] = np.concatenate([to_cos, to_sin], axis=1)
-    tables["col_back"] = np.concatenate([tables["col_cos"].T, tables["col_sin"].T], axis=1)
+    tables["col_back"] = np.concatenate([col_cos.T, col_sin.T], axis=1)
     place = np.zeros((parts, SUB, chans))
     for c in range(chans):
         place[c, :, c] = 1.0
@@ -317,36 +308,44 @@
 
 
 def columns_kernel(
-    in_hbm, pre_hbm, cot_hbm, time_hbm, col_hbm, square_hbm, swap_hbm, tile_hbm, sums_hbm,
-    out_ref, grad_ref, square_ref, swap_ref, tile_ref, sums_ref,
-    in_ref, pre_ref, cot_ref, time_ref, col_ref, sems,
+    in_hbm, pre_hbm, cot_hbm, time_hbm, col_hbm, square_hbm, swap_hbm, mixing_hbm, sums_hbm, place_hbm,
+    out_ref, grad_ref, square_ref, swap_ref, mixing_ref, sums_ref, place_ref,
+    in_ref, pre_ref, cot_ref, time_ref, col_ref, sems, *, chans,
 ):
     copies = start_copies(
         sems,
         (pre_hbm, pre_ref), (cot_hbm, cot_ref), (in_hbm, in_ref), (time_hbm, time_ref), (col_hbm, col_ref),
-        (square_hbm, square_ref), (swap_hbm, swap_ref), (tile_hbm, tile_ref), (sums_hbm, sums_ref),
+        (square_hbm, square_ref), (swap_hbm, swap_ref),
+        (mixing_hbm, mixing_ref), (sums_hbm, sums_ref), (place_hbm, place_ref),
     )
     rows, cols, width = in_ref.shape
-    copies[0].wait()
+    for copy in copies[:5]:
+        copy.wait()
     slopes = gelu_slope(pre_ref[...].reshape(rows * cols, width).astype(jnp.float32))
-    copies[1].wait()
     grad = (cot_ref[...].reshape(rows * cols, width).astype(jnp.float32) * slopes).astype(BF)
     grad_ref[...] = grad
-    copies[2].wait()
-    copies[3].wait()
     field = in_ref[...].reshape(rows * cols, width)
-    base, last_in, last_grad = [time_ref[i * width : (i + 1) * width] for i in range(3)]
-    time_in = dot(field, base)
-    time_grad = dot(grad, base)
-    last = dot(field, last_in) + dot(grad, last_grad)
-    in_re, in_im = time_in[:, :LANES], time_in[:, LANES:]
-    gr_re, gr_im = time_grad[:, :LANES], time_grad[:, LANES:]
-    direct = jnp.concatenate([in_re, in_im, gr_re, gr_im, last[:, :LANES]], axis=1).astype(BF)
-    turned = jnp.concatenate([in_im, -in_re, gr_im, -gr_re, last[:, LANES:]], axis=1).astype(BF)
-    copies[4].wait()
-    half = col_ref.shape[0] // 2
-    modes = dot(col_ref[:half], direct) + dot(col_ref[half:], turned)
-    out_ref[...] = pack(lane_blocks(modes))
+    times = jnp.concatenate([dot(field, time_ref[...]), dot(grad, time_ref[...])], axis=1).astype(BF)
+    col = col_ref[...]
+    row = lax.broadcasted_iota(jnp.int32, col.shape, 0) % rows
+    across = jnp.concatenate([jnp.where(row == r, col, jnp.zeros_like(col)) for r in range(rows)], axis=1)
+    waves = dot(across, times)
+    half = waves.shape[0] // 2
+    in_cos, in_cos2, gr_cos, gr_cos2 = lane_blocks(waves[:half])
+    in_sin, in_sin2, gr_sin, gr_sin2 = lane_blocks(waves[half:])
+    alone = lane_group(in_cos.shape, chans) == 0
+    last = jnp.where(alone, in_cos2, 0.0)
+    for place, part in enumerate((-in_sin2, gr_cos2, -gr_sin2)):
+        last = last + pltpu.roll(jnp.where(alone, part, 0.0), (place + 1) * chans, 1)
+    out_ref[...] = pack(
+        [
+            in_cos + jnp.where(alone, 0.0, in_sin2),
+            jnp.where(alone, 0.0, in_cos2) - in_sin,
+            gr_cos + jnp.where(alone, 0.0, gr_sin2),
+            jnp.where(alone, 0.0, gr_cos2) - gr_sin,
+            last,
+        ]
+    )
     for copy in copies[5:]:
         copy.wait()
 
@@ -367,9 +366,11 @@
     return dot(place, halves(folded, chans).astype(BF))
 
 
-def mixing_kernel(sent_hbm, grad_hbm, long_hbm, bypass_ref, spread_ref, mixed_ref, long_ref, grad_ref, sems):
+def mixing_kernel(
+    sent_hbm, grad_hbm, long_hbm, first_hbm, bypass_ref, spread_ref, mixed_ref, long_ref, first_ref, grad_ref, sems
+):
     del sent_hbm
-    copies = start_copies(sems, (grad_hbm, grad_ref), (long_hbm, long_ref))
+    copies = start_copies(sems, (grad_hbm, grad_ref), (long_hbm, long_ref), (first_hbm, first_ref))
     chans = bypass_ref.shape[0]
     spread = spread_ref[...]
     across = lax.dot_general(
@@ -378,10 +379,12 @@
     matrix = diagonal(dot(spread, across), chans).astype(BF)
     copies[0].wait()
     mixed_ref[...] = dot(grad_ref[...], matrix)
-    copies[1].wait()
-
-
-def rows_kernel(in_ref, square_ref, swap_ref, out_ref):
+    for copy in copies[1:]:
+        copy.wait()
+
+
+def rows_kernel(in_ref, square_ref, swap_ref, weight_hbm, out_ref):
+    del weight_hbm
     in_re, in_im, gr_re, gr_im, last = unpack(in_ref[...], 5)
     size = square_ref.shape[1]
     turned_last = dot(last, swap_ref[...]).astype(BF)
@@ -391,30 +394,37 @@
     out_ref[...] = pack(lane_blocks(modes))
 
 
+def mixing_tables(table_ref):
+    size = table_ref.shape[1]
+    tiles = [table_ref[2 * size + i * LANES : 2 * size + (i + 1) * LANES] for i in range(3)]
+    return table_ref[:size], table_ref[size : 2 * size], *tiles
+
+
 def back_kernel(
-    in_ref, grad_ref, weight_ref, field_ref, square_ref, tile_ref, sums_ref, place_ref, out_ref, modes_ref,
-    *, factor,
+    in_ref, grad_ref, weight_ref, field_ref, table_ref, sums_ref, place_ref, repeat_hbm, rows_hbm,
+    out_ref, modes_ref, repeat_ref, rows_ref, sems, *, factor,
 ):
     chans = place_ref.shape[1]
-    size = square_ref.shape[1]
+    copies = start_copies(sems, (rows_hbm, rows_ref), (repeat_hbm, repeat_ref))
+    size = table_ref.shape[1]
+    order, unorder, tile_a, tile_b, tile_last = mixing_tables(table_ref)
     lanes = jnp.concatenate(unpack(in_ref[...], 5), axis=1)
-    modes = dot(square_ref[4 * size : 5 * size], lanes).astype(BF)
+    modes = dot(order, lanes).astype(BF)
     modes_ref[...] = modes
-    rows, cols, width = field_ref.shape
-    terms = bypass_terms(field_ref[...].reshape(rows * cols, width), grad_ref[...], place_ref[...], chans)
     steps = weight_ref.shape[2]
     wide = weight_ref.shape[4]
     lead = LANES // chans
     gr_re, gr_im, last = lane_blocks(modes)[2:]
-    first = jnp.concatenate([gr_re, gr_im], axis=0)
+    first = jnp.concatenate([gr_re, gr_im], axis=1)
+    blank = jnp.zeros((LANES, LANES), BF)
+    tiles = [
+        jnp.concatenate([jnp.concatenate([t, blank], axis=1), jnp.concatenate([blank, t], axis=1)], axis=0)
+        for t in lane_blocks(tile_a) + lane_blocks(tile_b)
+    ]
     group = lane_group((size, LANES), chans)
     re_sum = im_sum = jnp.zeros((size, LANES), jnp.float32)
     for k in range(steps):
-        if k < lead:
-            g_both = dot(first, tile_ref[k]).astype(BF)
-            g_re, g_im = g_both[:size], g_both[size:]
-        else:
-            g_re, g_im = dot(last, tile_ref[lead]).astype(BF), dot(last, tile_ref[lead + 1]).astype(BF)
+        g_re, g_im = lane_blocks((dot(first, tiles[k]) if k < lead else dot(last, tile_last)).astype(BF))
         p_re, p_im = [], []
         for j in range(wide // LANES):
             w_re = weight_ref[0, :, k, :, j * LANES : (j + 1) * LANES].reshape(size, LANES)
@@ -428,40 +438,54 @@
             im_sum = jnp.where(group == k, summed[size:], im_sum)
         else:
             last_sum = jnp.where(group == 0, summed[:size], jnp.where(group == 1, summed[size:], 0.0))
+    rows, cols, width = field_ref.shape
+    terms = bypass_terms(field_ref[...].reshape(rows * cols, width), grad_ref[...], place_ref[...], chans)
     back = (jnp.concatenate([re_sum, im_sum, last_sum], axis=1) * factor).astype(BF)
-    re, im, last = lane_blocks(dot(square_ref[5 * size : 6 * size], back))
+    re, im, last = lane_blocks(dot(unorder, back))
     out_ref[...] = pack([re, im, last + terms])
-
-
-def weight_kernel(modes_ref, repeat_ref, tile_ref, out_ref, *, factor):
-    modes = modes_ref[...]
-    in_re, in_im, gr_re, gr_im, last = [modes[:, i * LANES : (i + 1) * LANES] for i in range(5)]
-    steps = out_ref.shape[2]
-    lead = tile_ref.shape[0] - 2
-    wide = out_ref.shape[-1]
+    for copy in copies:
+        copy.wait()
+
+
+def weight_kernel(modes_ref, repeat_ref, table_ref, out_hbm, out_ref, sems, *, factor):
+    slots, _, kept, count, wide = out_ref.shape
+    steps = out_hbm.shape[2]
+    lead = repeat_ref.shape[0] - 2
+    in_re, in_im, gr_re, gr_im, last = lane_blocks(modes_ref[...])
+    _, _, tile_a, tile_b, tile_last = mixing_tables(table_ref)
+    tiled = [lane_blocks(dot(g, tile_a) * factor) + lane_blocks(dot(g, tile_b) * factor) for g in (gr_re, gr_im)]
+    tiled = list(zip(*tiled)) + [lane_blocks(dot(last, tile_last) * factor)]
+    copies = []
     for k in range(steps):
         if k < lead:
             a_re, a_im = dot(in_re, repeat_ref[k]), dot(in_im, repeat_ref[k])
-            b_re, b_im = dot(gr_re, tile_ref[k]), dot(gr_im, tile_ref[k])
         else:
             a_re, a_im = dot(last, repeat_ref[lead]), dot(last, repeat_ref[lead + 1])
-            b_re, b_im = dot(last, tile_ref[lead]), dot(last, tile_ref[lead + 1])
-        b_re = jnp.concatenate([b_re * factor] * (wide // LANES), axis=1)
-        b_im = jnp.concatenate([b_im * factor] * (wide // LANES), axis=1)
-        out_ref[0, 0, k] = a_re * b_re + a_im * b_im
-        out_ref[1, 0, k] = a_re * b_im - a_im * b_re
-
-
-def rows_back_kernel(in_ref, square_ref, swap_ref, out_ref, *, chans):
+        b_re, b_im = tiled[k]
+        slot = k % slots
+        if k >= slots:
+            copies[k - slots].wait()
+        for j in range(wide // LANES):
+            part = slice(j * LANES, (j + 1) * LANES)
+            out_ref[slot, 0, :, :, part] = (a_re[:, part] * b_re + a_im[:, part] * b_im).reshape(kept, count, LANES)
+            out_ref[slot, 1, :, :, part] = (a_re[:, part] * b_im - a_im[:, part] * b_re).reshape(kept, count, LANES)
+        copies.append(pltpu.make_async_copy(out_ref.at[slot], out_hbm.at[:, :, k], sems.at[slot]))
+        copies[k].start()
+    for copy in copies[max(0, steps - slots) :]:
+        copy.wait()
+
+
+def rows_back_kernel(in_ref, table_ref, swap_ref, out_ref, *, chans):
     re, im, tail = unpack(in_ref[...], 3)
-    size = square_ref.shape[1]
+    size = table_ref.shape[1]
+    back_cos, back_sin, total = [table_ref[i * size : (i + 1) * size] for i in range(3)]
     group = lane_group(tail.shape, chans)
     last = jnp.where(group < 2, tail.astype(jnp.float32), 0.0).astype(BF)
     turned_last = dot(-last, swap_ref[...]).astype(BF)
     direct = jnp.concatenate([re, im, last], axis=1)
     turned = jnp.concatenate([-im, re, turned_last], axis=1)
-    rows = dot(square_ref[2 * size : 3 * size], direct) + dot(square_ref[3 * size : 4 * size], turned)
-    summed = dot(square_ref[6 * size : 7 * size], tail)
+    rows = dot(back_cos, direct) + dot(back_sin, turned)
+    summed = dot(total, tail)
     summed = summed + pltpu.roll(summed, LANES - chans, 1)
     summed = jnp.where(group == 2, summed, 0.0)
     summed = summed + pltpu.roll(summed, chans, 1)
@@ -469,10 +493,9 @@
     out_ref[...] = pack([re, im, last + halves(summed, chans)])
 
 
-def columns_back_kernel(in_ref, mixed_ref, square_ref, long_ref, out_ref, bypass_ref, *, factor):
+def columns_back_kernel(in_ref, mixed_ref, first_ref, long_ref, out_ref, bypass_ref, *, factor):
     rows, cols, width = out_ref.shape
     chans = bypass_ref.shape[0]
-    size = square_ref.shape[1]
     blocks = unpack(in_ref[...], 3)
     lanes = jnp.concatenate(blocks, axis=1)
     height = lanes.shape[1]
@@ -480,7 +503,7 @@
     stacked = jnp.concatenate([steps[:, :width], steps[:, width:]], axis=0)
     total = dot(long_ref[height:], stacked) + mixed_ref[...]
     out_ref[...] = total.reshape(rows, cols, width).astype(BF)
-    sums = dot(square_ref[7 * size :], blocks[2])
+    sums = dot(first_ref[...], blocks[2])
     sums = pltpu.roll(sums + pltpu.roll(sums, LANES - chans, 1), LANES // 2, 1)
     bypass_ref[...] = sums[:, :chans] * factor
 
@@ -510,13 +533,17 @@
     factor = 1.0 / math.sqrt(float(total_x * cols * steps * row_modes * col_modes * time_modes))
     bypass_factor = 1.0 / math.sqrt(float(total_x * cols * steps))
     tables = build_tables(parts, rows, cols, steps, chans, row_modes, pair, kept, col_modes, time_modes)
-    stack = lambda *names: jnp.asarray(np.concatenate([tables[name] for name in names], axis=0))
-    time_table = stack("time_base", "time_last_in", "time_last_grad")
-    col_table = stack("col_cos", "col_sin")
-    square = stack("row_cos", "row_sin", "back_cos", "back_sin", "order", "unorder", "total", "first")
+    stack_all = lambda arrays: jnp.asarray(np.concatenate(arrays, axis=0))
+    stack = lambda *names: stack_all([tables[name] for name in names])
+    square = stack("row_cos", "row_sin")
+    mixing = stack_all(
+        [tables["order"], tables["unorder"]] + np.split(tables["tile"], 2, axis=1) + [tables["tile_last"]]
+    )
+    back_table = stack("back_cos", "back_sin", "total")
     long = stack("time_back", "col_back")
-    swap, tile, repeat, sums, spread, place = [
-        jnp.asarray(tables[name]) for name in ("swap", "tile", "repeat", "sums", "spread_chan", "place")
+    time_table, col_table, swap, repeat, sums, spread, place, first = [
+        jnp.asarray(tables[name])
+        for name in ("time", "col", "swap", "repeat", "sums", "spread_chan", "place", "first")
     ]
 
     def swap_parts(array):
@@ -526,46 +553,52 @@
     shape = jax.ShapeDtypeStruct
     chunk = parts * SUB
     field = (rows * cols, width)
-    sent, pre_grad, square, swap, tile, sums = call(
-        columns_kernel,
-        (shape((5 * chunk, LANES), BF), shape(field, BF)) + tuple(like(a) for a in (square, swap, tile, sums)),
-        inputs, preactivation, cotangent, time_table, col_table, square, swap, tile, sums,
-        far=range(9),
+    sent, pre_grad, square, swap, mixing, sums, place = call(
+        lambda *refs: columns_kernel(*refs, chans=chans),
+        (shape((5 * chunk, LANES), BF), shape(field, BF))
+        + tuple(like(a) for a in (square, swap, mixing, sums, place)),
+        inputs, preactivation, cotangent, time_table, col_table, square, swap, mixing, sums, place,
+        far=range(10),
         scratch=[pltpu.VMEM(a.shape, a.dtype) for a in (inputs, inputs, inputs, time_table, col_table)]
-        + [pltpu.SemaphoreType.DMA((9,))],
-    )
-    sent = call(rows_kernel, shape((5 * chunk, LANES), BF), swap_parts(sent), square, swap)
+        + [pltpu.SemaphoreType.DMA((10,))],
+    )
     weight = spectral.transpose(0, 1, 3, 2, 4)
-    sent, modes = call(
+    sent = call(rows_kernel, shape((5 * chunk, LANES), BF), swap_parts(sent), square, swap, weight, far=(3,))
+    sent, modes, repeat, back_table = call(
         lambda *refs: back_kernel(*refs, factor=factor),
-        (shape((3 * chunk, LANES), BF), shape((kept * col_modes, 5 * LANES), BF)),
-        swap_parts(sent), pre_grad, weight, inputs, square, tile, sums, place,
-    )
-    whole = lambda a: pl.BlockSpec(a.shape, lambda i: (0,) * a.ndim)
+        (shape((3 * chunk, LANES), BF), shape((kept * col_modes, 5 * LANES), BF), like(repeat), like(back_table)),
+        swap_parts(sent), pre_grad, weight, inputs, mixing, sums, place, repeat, back_table,
+        far=(7, 8),
+        scratch=[pltpu.SemaphoreType.DMA((2,))],
+    )
+    near = pl.BlockSpec(memory_space=pltpu.VMEM)
+    slots = 3
     grad_spectral = pl.pallas_call(
         lambda *refs: weight_kernel(*refs, factor=factor),
-        grid=(kept,),
         out_shape=shape((2, kept, time_modes, col_modes, wide), jnp.float32),
-        in_specs=[pl.BlockSpec((col_modes, 5 * LANES), lambda i: (i, 0)), whole(repeat), whole(tile)],
-        out_specs=pl.BlockSpec((2, 1, time_modes, col_modes, wide), lambda i: (0, i, 0, 0, 0)),
+        in_specs=[near, near, near],
+        out_specs=pl.BlockSpec(memory_space=pltpu.HBM),
+        scratch_shapes=[
+            pltpu.VMEM((slots, 2, kept, col_modes, wide), jnp.float32), pltpu.SemaphoreType.DMA((slots,)),
+        ],
         compiler_params=pltpu.CompilerParams(vmem_limit_bytes=16 * 1024 * 1024),
-    )(modes, repeat, tile).transpose(0, 1, 3, 2, 4)
+    )(*[pltpu.with_memory_space_constraint(a, pltpu.VMEM) for a in (modes, repeat, mixing)]).transpose(0, 1, 3, 2, 4)
     sent = call(
         lambda *refs: rows_back_kernel(*refs, chans=chans),
         shape((3 * chunk, LANES), BF),
-        swap_parts(sent), square, swap,
-    )
-    mixed, long = call(
+        swap_parts(sent), back_table, swap,
+    )
+    mixed, long, first = call(
         mixing_kernel,
-        (shape(field, jnp.float32), like(long)),
-        sent, pre_grad, long, bypass, spread,
-        far=(0, 1, 2),
-        scratch=[pltpu.VMEM(field, BF), pltpu.SemaphoreType.DMA((2,))],
+        (shape(field, jnp.float32), like(long), like(first)),
+        sent, pre_grad, long, first, bypass, spread,
+        far=(0, 1, 2, 3),
+        scratch=[pltpu.VMEM(field, BF), pltpu.SemaphoreType.DMA((3,))],
     )
     grad_inputs, grad_bypass = call(
         lambda *refs: columns_back_kernel(*refs, factor=bypass_factor),
         (shape((rows, cols, width), BF), shape((chans, chans), jnp.float32)),
-        swap_parts(sent), mixed, square, long,
+        swap_parts(sent), mixed, first, long,
         keep=False,
     )
     return (grad_inputs, grad_spectral, grad_bypass)

time: 66.1 us -> 64.9 us (0.982)
  Pallas kernels: 15.9 us -> 14.3 us
    pallas_call x6, Pallas kernels: 10.2 us -> 9.07 us  [call(): pl.pallas_call(kernel, out_shape=jax.tree.map(hold, out_shapes), in_specs...]
  transfers between devices with their start and end apart: 1 -> 1, of which waited for: 1 -> 1; matrix products, arithmetic and copies ran while one was open for 0% -> 0% of each run, Pallas kernels for 11% -> 10%
where the time goes in v2:
time: 64.9 us; the launch traced here: 64.6 us
  blocking collectives  44.6 us (69%)
  Pallas kernels  14.3 us (22%)
  waiting for transfers between devices  2.66 us (4%)
  starting transfers between devices  2.37 us (4%)
  between operations  0.74 us (1%)
    all_to_all x3, blocking collectives, swap_parts(): return lax.all_to_all(array, 'row', 0, 0, tiled=True)  44.6 us
    pallas_call x6, Pallas kernels, call(): pl.pallas_call(kernel, out_shape=jax.tree.map(hold, out_shapes), in_specs...  9.07 us
    pallas_call x1, Pallas kernels, local(): pl.pallas_call(lambda *refs: weight_kernel(*refs, factor=factor), out_sha...  5.21 us
    all_to_all x1, waiting for transfers between devices, swap_parts(): return lax.all_to_all(array, 'row', 0, 0, tiled=True)  2.66 us
    all_to_all x1, starting transfers between devices, swap_parts(): return lax.all_to_all(array, 'row', 0, 0, tiled=True)  2.37 us
  transfers between devices with their start and end apart: 1, of which 1 were waited for; matrix products, arithmetic and copies ran while one was open for 0% of the time, Pallas kernels for 10%

profile of v2, /device:TPU:1, one launch (start us, length us, event | category | flops | bytes accessed | tf_op | source)
XLA Modules:
  0.0 64.6 jit_solution(3887379700816817976)
XLA Ops:
  0.6 0.0 copy-start.2
  0.6 0.0 copy-start
  0.7 2.2 %shard_map.184 = (bf16[1280,128]{1,0:T(8,128)(2,1)S(1)}, bf16[512,256]{1,0:T(8,128)(2,1)S(1)}, bf16[512,256]{1,0:T(8,128)(2,1)S(1)}, bf16[128,128]{1,0:T(8,128)(...) custom-call(bf16[4,128,256]{2,1,0:T(8,128)(2,1)} %refs_3_.2, ...), custom_call_target="tpu_custom_call" | custom-call | tf_op jit(solution)/shard_map/pallas_call | solution.py:263
  2.9 0.0 copy-start.1
  2.9 18.2 %all_to_all.44 = bf16[32,40,128]{2,1,0:T(8,128)(2,1)S(1)} all-to-all(bf16[32,40,128]{2,1,0:T(8,128)(2,1)S(1)} %bitcast.17), channel_id=1, replica_groups=mesh['row'=32,'col'=1] {'row'}, dimensions={0} | all-to-all | bytes 655360 | tf_op jit(solution)/shard_map/all_to_all | solution.py:550
  21.1 0.4 shard_map.185
  21.5 14.2 %all_to_all.45 = bf16[32,40,128]{2,1,0:T(8,128)(2,1)S(1)} all-to-all(bf16[32,40,128]{2,1,0:T(8,128)(2,1)S(1)} %bitcast.14), channel_id=1, replica_groups=mesh['row'=32,'col'=1] {'row'}, dimensions={0} | all-to-all | bytes 655360 | tf_op jit(solution)/shard_map/all_to_all | solution.py:550
  35.7 0.0 copy-done.2
  35.7 0.0 copy-done
  35.7 2.7 %shard_map.186 = (bf16[768,128]{1,0:T(8,128)(2,1)S(1)}, bf16[256,640]{1,0:T(8,128)(2,1)S(1)}, bf16[6,128,1024]{2,1,0:T(8,128)(2,1)S(1)}, bf16[768,256]{1,0:T(8,128)(2,1)S(1)}) custom-call(bf16[1280,128]{1,0:T(8,128)(2,1)S(1)} %bitcast.12, bf16[512,256]{1,0:T(8,128)(2,1)S(1)} %get-tuple-element.22.refs_1_.grad_hbm, bf16[2,4,5,64,1024]{4,3,2,1,0:T(8,128)(2,1)S(1)} %bitcast.11, ...), custom_call_target="tpu_custom_call" | custom-call | tf_op jit(solution)/shard_map/pallas_call | solution.py:263
  38.4 0.0 copy-done.1
  38.4 12.2 %all_to_all.46 = bf16[32,24,128]{2,1,0:T(8,128)(2,1)S(1)} all-to-all(bf16[32,24,128]{2,1,0:T(8,128)(2,1)S(1)} %bitcast.18), channel_id=1, replica_groups=mesh['row'=32,'col'=1] {'row'}, dimensions={0} | all-to-all | bytes 393216 | tf_op jit(solution)/shard_map/all_to_all | solution.py:550
  50.6 1.2 %shard_map.187.sent_hbm = bf16[768,128]{1,0:T(8,128)(2,1)} custom-call(bf16[768,128]{1,0:T(8,128)(2,1)S(1)} %bitcast.16, bf16[768,256]{1,0:T(8,128)(2,1)S(1)} %get-tuple-element.27.refs_1_, bf16[128,128]{1,0:T(8,128)(2,1)S(1)} %get-tuple-element.21.swap_ref.refs_2_), custom_call_target="tpu_custom_call" | custom-call | tf_op jit(solution)/shard_map/pallas_call | solution.py:263
  51.7 2.4 %all-to-all-start.3 = ((bf16[32,24,128]{2,1,0:T(8,128)(2,1)}), bf16[32,24,128]{2,1,0:T(8,128)(2,1)S(1)}, u32[]{:S(2)}, u32[]{:S(2)}) async-start(bf16[32,24,128]{2,1,0:T(8,128)(2,1)} %bitcast.7), calls=%async_computation.3 | async-start | bytes 393216 | tf_op jit(solution)/shard_map/all_to_all | solution.py:550
  54.1 0.0 copy-start.3
  54.1 0.0 copy-start.4
  54.1 5.2 %shard_map.190 = f32[2,4,5,64,1024]{4,3,2,1,0:T(8,128)} custom-call(bf16[256,640]{1,0:T(8,128)(2,1)S(1)} %get-tuple-element.32.refs_0_, bf16[6,128,1024]{2,1,0:T(8,128)(2,1)S(1)} %get-tuple-element.33.refs_1_, bf16[896,256]{1,0:T(8,128)(2,1)S(1)} %get-tuple-element.23.refs_4_.refs_2_), custom_call_target="tpu_custom_call" | custom-call | tf_op jit(solution)/shard_map/pallas_call | solution.py:576
  59.3 0.0 copy-done.3
  59.4 0.0 copy-done.4
  59.4 1.3 %shard_map.188 = (f32[512,256]{1,0:T(8,128)S(1)}, bf16[896,512]{1,0:T(8,128)(2,1)S(1)}, bf16[32,256]{1,0:T(8,128)(2,1)S(1)}) custom-call(bf16[768,128]{1,0:T(8,128)(2,1)} %shard_map.187.sent_hbm, bf16[512,256]{1,0:T(8,128)(2,1)} %copy-done.1, bf16[896,512]{1,0:T(8,128)(2,1)} %constant.27.clone.long_hbm, bf16[32,256]{1,0:T(8,128)(2,1)} %constant.35.clone.first_hbm, ...), custom_call_target="tpu_custom_call" | custom-call | tf_op jit(solution)/shard_map/pallas_call | solution.py:263
  60.7 2.7 %all-to-all-done.3 = bf16[32,24,128]{2,1,0:T(8,128)(2,1)S(1)} async-done(((bf16[32,24,128]{2,1,0:T(8,128)(2,1)}), bf16[32,24,128]{2,1,0:T(8,128)(2,1)S(1)}, u32[]{:S(2)}, u32[]{:S(2)}) %all-to-all-start.3) | async-done | bytes 196640 | tf_op jit(solution)/shard_map/all_to_all | solution.py:550
  63.3 1.3 %shard_map.189 = (bf16[4,128,256]{2,1,0:T(8,128)(2,1)}, f32[32,32]{1,0:T(8,128)}) custom-call(bf16[768,128]{1,0:T(8,128)(2,1)S(1)} %bitcast.15, f32[512,256]{1,0:T(8,128)S(1)} %get-tuple-element.28.refs_1_, bf16[32,256]{1,0:T(8,128)(2,1)S(1)} %get-tuple-element.29.refs_2_, bf16[896,512]{1,0:T(8,128)(2,1)S(1)} %get-tuple-element.30.refs_3_), custom_call_target="tpu_custom_call" | custom-call | tf_op jit(solution)/shard_map/pallas_call | solution.py:263
Async XLA Ops:
  0.6 35.1 %copy-start.2 = (bf16[4,128,256]{2,1,0:T(8,128)(2,1)S(1)}, bf16[4,128,256]{2,1,0:T(8,128)(2,1)}, u32[]{:S(2)}) copy-start(bf16[4,128,256]{2,1,0:T(8,128)(2,1)} %refs_3_.2) | copy-start | bytes 786436
  0.6 35.1 %copy-start = (bf16[2,4,64,5,1024]{4,2,3,1,0:T(8,128)(2,1)S(1)}, bf16[2,4,64,5,1024]{4,2,3,1,0:T(8,128)(2,1)}, u32[]{:S(2)}) copy-start(bf16[2,4,64,5,1024]{4,2,3,1,0:T(8,128)(2,1)} %param.20) | copy-start | bytes 15728644
  2.9 35.5 %copy-start.1 = (bf16[512,256]{1,0:T(8,128)(2,1)}, bf16[512,256]{1,0:T(8,128)(2,1)S(1)}, u32[]{:S(2)}) copy-start(bf16[512,256]{1,0:T(8,128)(2,1)S(1)} %get-tuple-element.22.refs_1_.grad_hbm) | copy-start | bytes 786436
  51.7 11.6 %all-to-all-start.3 = ((bf16[32,24,128]{2,1,0:T(8,128)(2,1)}), bf16[32,24,128]{2,1,0:T(8,128)(2,1)S(1)}, u32[]{:S(2)}, u32[]{:S(2)}) async-start(bf16[32,24,128]{2,1,0:T(8,128)(2,1)} %bitcast.7), calls=%async_computation.3 | async-start | bytes 393216 | tf_op jit(solution)/shard_map/all_to_all | solution.py:550
  54.1 5.2 %copy-start.3 = (bf16[256,32]{1,0:T(8,128)(2,1)S(1)}, bf16[256,32]{1,0:T(8,128)(2,1)}, u32[]{:S(2)}) copy-start(bf16[256,32]{1,0:T(8,128)(2,1)} %constant.33.clone.spread_ref) | copy-start | bytes 49156
  54.1 5.2 %copy-start.4 = (bf16[32,32]{1,0:T(8,128)(2,1)S(1)}, bf16[32,32]{1,0:T(8,128)(2,1)}, u32[]{:S(2)}) copy-start(bf16[32,32]{1,0:T(8,128)(2,1)} %bypass_ref.1) | copy-start | bytes 6148

commit v3 on v2

--- a/solution.py
+++ b/solution.py
@@ -209,8 +209,6 @@
     tables["row_sin"] = spread(sin_x)
     tables["back_cos"] = spread(cos_x).T
     tables["back_sin"] = spread(sin_x).T
-    swap = np.kron(np.array([[0.0, -1.0], [1.0, 0.0]]), eye)
-    tables["swap"] = np.kron(np.eye(LANES // (2 * chans)), swap)
     order = np.zeros((kept, col_modes, parts, pair, kept))
     for k in range(kept):
         for e in range(parts):
@@ -308,15 +306,14 @@
 
 
 def columns_kernel(
-    in_hbm, pre_hbm, cot_hbm, time_hbm, col_hbm, square_hbm, swap_hbm, mixing_hbm, sums_hbm, place_hbm,
-    out_ref, grad_ref, square_ref, swap_ref, mixing_ref, sums_ref, place_ref,
+    in_hbm, pre_hbm, cot_hbm, time_hbm, col_hbm, square_hbm,
+    out_ref, grad_ref, square_ref,
     in_ref, pre_ref, cot_ref, time_ref, col_ref, sems, *, chans,
 ):
     copies = start_copies(
         sems,
         (pre_hbm, pre_ref), (cot_hbm, cot_ref), (in_hbm, in_ref), (time_hbm, time_ref), (col_hbm, col_ref),
-        (square_hbm, square_ref), (swap_hbm, swap_ref),
-        (mixing_hbm, mixing_ref), (sums_hbm, sums_ref), (place_hbm, place_ref),
+        (square_hbm, square_ref),
     )
     rows, cols, width = in_ref.shape
     for copy in copies[:5]:
@@ -383,11 +380,16 @@
         copy.wait()
 
 
-def rows_kernel(in_ref, square_ref, swap_ref, weight_hbm, out_ref):
+def quarter_turn(values, chans):
+    ahead, behind = pltpu.roll(values, LANES - chans, 1), pltpu.roll(values, chans, 1)
+    return jnp.where(lane_group(values.shape, chans) % 2 == 0, ahead, -behind)
+
+
+def rows_kernel(in_ref, square_ref, weight_hbm, out_ref, *, chans):
     del weight_hbm
     in_re, in_im, gr_re, gr_im, last = unpack(in_ref[...], 5)
     size = square_ref.shape[1]
-    turned_last = dot(last, swap_ref[...]).astype(BF)
+    turned_last = quarter_turn(last.astype(jnp.float32), chans).astype(BF)
     direct = jnp.concatenate([in_re, in_im, gr_re, gr_im, last], axis=1)
     turned = jnp.concatenate([in_im, -in_re, gr_im, -gr_re, turned_last], axis=1)
     modes = dot(square_ref[:size], direct) + dot(square_ref[size : 2 * size], turned)
@@ -475,13 +477,14 @@
         copy.wait()
 
 
-def rows_back_kernel(in_ref, table_ref, swap_ref, out_ref, *, chans):
+def rows_back_kernel(in_ref, table_ref, out_ref, *, chans):
     re, im, tail = unpack(in_ref[...], 3)
     size = table_ref.shape[1]
     back_cos, back_sin, total = [table_ref[i * size : (i + 1) * size] for i in range(3)]
     group = lane_group(tail.shape, chans)
-    last = jnp.where(group < 2, tail.astype(jnp.float32), 0.0).astype(BF)
-    turned_last = dot(-last, swap_ref[...]).astype(BF)
+    last = jnp.where(group < 2, tail.astype(jnp.float32), 0.0)
+    turned_last = -quarter_turn(last, chans).astype(BF)
+    last = last.astype(BF)
     direct = jnp.concatenate([re, im, last], axis=1)
     turned = jnp.concatenate([-im, re, turned_last], axis=1)
     rows = dot(back_cos, direct) + dot(back_sin, turned)
@@ -541,9 +544,9 @@
     )
     back_table = stack("back_cos", "back_sin", "total")
     long = stack("time_back", "col_back")
-    time_table, col_table, swap, repeat, sums, spread, place, first = [
+    time_table, col_table, repeat, sums, spread, place, first = [
         jnp.asarray(tables[name])
-        for name in ("time", "col", "swap", "repeat", "sums", "spread_chan", "place", "first")
+        for name in ("time", "col", "repeat", "sums", "spread_chan", "place", "first")
     ]
 
     def swap_parts(array):
@@ -553,17 +556,22 @@
     shape = jax.ShapeDtypeStruct
     chunk = parts * SUB
     field = (rows * cols, width)
-    sent, pre_grad, square, swap, mixing, sums, place = call(
+    sent, pre_grad, square = call(
         lambda *refs: columns_kernel(*refs, chans=chans),
         (shape((5 * chunk, LANES), BF), shape(field, BF))
-        + tuple(like(a) for a in (square, swap, mixing, sums, place)),
-        inputs, preactivation, cotangent, time_table, col_table, square, swap, mixing, sums, place,
-        far=range(10),
+        + (like(square),),
+        inputs, preactivation, cotangent, time_table, col_table, square,
+        far=range(6),
         scratch=[pltpu.VMEM(a.shape, a.dtype) for a in (inputs, inputs, inputs, time_table, col_table)]
-        + [pltpu.SemaphoreType.DMA((10,))],
+        + [pltpu.SemaphoreType.DMA((6,))],
     )
     weight = spectral.transpose(0, 1, 3, 2, 4)
-    sent = call(rows_kernel, shape((5 * chunk, LANES), BF), swap_parts(sent), square, swap, weight, far=(3,))
+    sent = call(
+        lambda *refs: rows_kernel(*refs, chans=chans),
+        shape((5 * chunk, LANES), BF),
+        swap_parts(sent), square, weight,
+        far=(2,),
+    )
     sent, modes, repeat, back_table = call(
         lambda *refs: back_kernel(*refs, factor=factor),
         (shape((3 * chunk, LANES), BF), shape((kept * col_modes, 5 * LANES), BF), like(repeat), like(back_table)),
@@ -586,7 +594,7 @@
     sent = call(
         lambda *refs: rows_back_kernel(*refs, chans=chans),
         shape((3 * chunk, LANES), BF),
-        swap_parts(sent), back_table, swap,
+        swap_parts(sent), back_table,
     )
     mixed, long, first = call(
         mixing_kernel,

time: 64.9 us -> 65 us (level)
  no operation moved by 1% of the time
where the time goes in v3:
time: 65 us; the launch traced here: 64.7 us
  blocking collectives  44.6 us (69%)
  Pallas kernels  14.3 us (22%)
  waiting for transfers between devices  2.66 us (4%)
  starting transfers between devices  2.37 us (4%)
  between operations  0.79 us (1%)
    all_to_all x3, blocking collectives, swap_parts(): return lax.all_to_all(array, 'row', 0, 0, tiled=True)  44.6 us
    pallas_call x6, Pallas kernels, call(): pl.pallas_call(kernel, out_shape=jax.tree.map(hold, out_shapes), in_specs...  9.05 us
    pallas_call x1, Pallas kernels, local(): pl.pallas_call(lambda *refs: weight_kernel(*refs, factor=factor), out_sha...  5.2 us
    all_to_all x1, waiting for transfers between devices, swap_parts(): return lax.all_to_all(array, 'row', 0, 0, tiled=True)  2.66 us
    all_to_all x1, starting transfers between devices, swap_parts(): return lax.all_to_all(array, 'row', 0, 0, tiled=True)  2.37 us
  transfers between devices with their start and end apart: 1, of which 1 were waited for; matrix products, arithmetic and copies ran while one was open for 0% of the time, Pallas kernels for 10%

profile of v3, /device:TPU:1, one launch (start us, length us, event | category | flops | bytes accessed | tf_op | source)
XLA Modules:
  0.0 64.7 jit_solution(4298132442786288586)
XLA Ops:
  0.6 0.0 copy-start.1
  0.6 0.0 copy-start.5
  0.7 0.0 copy-start.4
  0.7 0.0 copy-start.2
  0.7 0.0 copy-start
  0.7 2.2 %shard_map.175 = (bf16[1280,128]{1,0:T(8,128)(2,1)S(1)}, bf16[512,256]{1,0:T(8,128)(2,1)S(1)}, bf16[512,256]{1,0:T(8,128)(2,1)S(1)}) custom-call(bf16[4,128,256]{2,1,0:T(8,128)(2,1)} %refs_3_.2, bf16[4,128,256]{2,1,0:T(8,128)(2,1)} %refs_1_.1, bf16[4,128,256]{2,1,0:T(8,128)(2,1)} %refs_2_.2, bf16[256,256]{1,0:T(8,128)(2,1)} %constant.26.clone.refs_3_, ...), custom_call_target="tpu_custom_call" | custom-call | tf_op jit(solution)/shard_map/pallas_call | solution.py:261
  2.9 0.0 copy-start.3
  2.9 18.2 %all_to_all.44 = bf16[32,40,128]{2,1,0:T(8,128)(2,1)S(1)} all-to-all(bf16[32,40,128]{2,1,0:T(8,128)(2,1)S(1)} %bitcast.17), channel_id=1, replica_groups=mesh['row'=32,'col'=1] {'row'}, dimensions={0} | all-to-all | bytes 655360 | tf_op jit(solution)/shard_map/all_to_all | solution.py:553
  21.1 0.4 shard_map.176
  21.4 14.2 %all_to_all.45 = bf16[32,40,128]{2,1,0:T(8,128)(2,1)S(1)} all-to-all(bf16[32,40,128]{2,1,0:T(8,128)(2,1)S(1)} %bitcast.14), channel_id=1, replica_groups=mesh['row'=32,'col'=1] {'row'}, dimensions={0} | all-to-all | bytes 655360 | tf_op jit(solution)/shard_map/all_to_all | solution.py:553
  35.7 0.0 copy-done.1
  35.7 0.0 copy-done.5
  35.7 0.0 copy-done.4
  35.7 0.0 copy-done.2
  35.7 0.0 copy-done
  35.7 2.7 %shard_map.177 = (bf16[768,128]{1,0:T(8,128)(2,1)S(1)}, bf16[256,640]{1,0:T(8,128)(2,1)S(1)}, bf16[6,128,1024]{2,1,0:T(8,128)(2,1)S(1)}, bf16[768,256]{1,0:T(8,128)(2,1)S(1)}) custom-call(bf16[1280,128]{1,0:T(8,128)(2,1)S(1)} %bitcast.12, bf16[512,256]{1,0:T(8,128)(2,1)S(1)} %get-tuple-element.17.refs_1_.grad_hbm, bf16[2,4,5,64,1024]{4,3,2,1,0:T(8,128)(2,1)S(1)} %bitcast.11, ...), custom_call_target="tpu_custom_call" | custom-call | tf_op jit(solution)/shard_map/pallas_call | solution.py:261
  38.4 0.0 copy-done.3
  38.4 12.2 %all_to_all.46 = bf16[32,24,128]{2,1,0:T(8,128)(2,1)S(1)} all-to-all(bf16[32,24,128]{2,1,0:T(8,128)(2,1)S(1)} %bitcast.18), channel_id=1, replica_groups=mesh['row'=32,'col'=1] {'row'}, dimensions={0} | all-to-all | bytes 393216 | tf_op jit(solution)/shard_map/all_to_all | solution.py:553
  50.5 1.2 %shard_map.178.sent_hbm = bf16[768,128]{1,0:T(8,128)(2,1)} custom-call(bf16[768,128]{1,0:T(8,128)(2,1)S(1)} %bitcast.16, bf16[768,256]{1,0:T(8,128)(2,1)S(1)} %get-tuple-element.19.refs_1_), custom_call_target="tpu_custom_call" | custom-call | tf_op jit(solution)/shard_map/pallas_call | solution.py:261
  51.8 2.4 %all-to-all-start.3 = ((bf16[32,24,128]{2,1,0:T(8,128)(2,1)}), bf16[32,24,128]{2,1,0:T(8,128)(2,1)S(1)}, u32[]{:S(2)}, u32[]{:S(2)}) async-start(bf16[32,24,128]{2,1,0:T(8,128)(2,1)} %bitcast.7), calls=%async_computation.3 | async-start | bytes 393216 | tf_op jit(solution)/shard_map/all_to_all | solution.py:553
  54.1 0.0 copy-start.6
  54.2 0.0 copy-start.7
  54.2 5.2 %shard_map.181 = f32[2,4,5,64,1024]{4,3,2,1,0:T(8,128)} custom-call(bf16[256,640]{1,0:T(8,128)(2,1)S(1)} %get-tuple-element.24.refs_0_, bf16[6,128,1024]{2,1,0:T(8,128)(2,1)S(1)} %get-tuple-element.25.refs_1_, bf16[896,256]{1,0:T(8,128)(2,1)S(1)} %copy-done.1), custom_call_target="tpu_custom_call" | custom-call | tf_op jit(solution)/shard_map/pallas_call | solution.py:584
  59.4 0.0 copy-done.6
  59.4 0.0 copy-done.7
  59.4 1.3 %shard_map.179 = (f32[512,256]{1,0:T(8,128)S(1)}, bf16[896,512]{1,0:T(8,128)(2,1)S(1)}, bf16[32,256]{1,0:T(8,128)(2,1)S(1)}) custom-call(bf16[768,128]{1,0:T(8,128)(2,1)} %shard_map.178.sent_hbm, bf16[512,256]{1,0:T(8,128)(2,1)} %copy-done.3, bf16[896,512]{1,0:T(8,128)(2,1)} %constant.25.clone.long_hbm, bf16[32,256]{1,0:T(8,128)(2,1)} %constant.32.clone.first_hbm, ...), custom_call_target="tpu_custom_call" | custom-call | tf_op jit(solution)/shard_map/pallas_call | solution.py:261
  60.7 2.7 %all-to-all-done.3 = bf16[32,24,128]{2,1,0:T(8,128)(2,1)S(1)} async-done(((bf16[32,24,128]{2,1,0:T(8,128)(2,1)}), bf16[32,24,128]{2,1,0:T(8,128)(2,1)S(1)}, u32[]{:S(2)}, u32[]{:S(2)}) %all-to-all-start.3) | async-done | bytes 196640 | tf_op jit(solution)/shard_map/all_to_all | solution.py:553
  63.4 1.3 %shard_map.180 = (bf16[4,128,256]{2,1,0:T(8,128)(2,1)}, f32[32,32]{1,0:T(8,128)}) custom-call(bf16[768,128]{1,0:T(8,128)(2,1)S(1)} %bitcast.15, f32[512,256]{1,0:T(8,128)S(1)} %get-tuple-element.20.refs_1_, bf16[32,256]{1,0:T(8,128)(2,1)S(1)} %get-tuple-element.21.refs_2_, bf16[896,512]{1,0:T(8,128)(2,1)S(1)} %get-tuple-element.22.refs_3_), custom_call_target="tpu_custom_call" | custom-call | tf_op jit(solution)/shard_map/pallas_call | solution.py:261
Async XLA Ops:
  0.6 35.0 %copy-start.1 = (bf16[896,256]{1,0:T(8,128)(2,1)S(1)}, bf16[896,256]{1,0:T(8,128)(2,1)}, u32[]{:S(2)}) copy-start(bf16[896,256]{1,0:T(8,128)(2,1)} %constant.23.clone.refs_4_.refs_2_) | copy-start | bytes 1376260
  0.6 35.0 %copy-start.5 = (bf16[256,32]{1,0:T(8,128)(2,1)S(1)}, bf16[256,32]{1,0:T(8,128)(2,1)}, u32[]{:S(2)}) copy-start(bf16[256,32]{1,0:T(8,128)(2,1)} %constant.31.clone.refs_6_) | copy-start | bytes 49156
  0.7 35.0 %copy-start.4 = (bf16[1024,128]{1,0:T(8,128)(2,1)S(1)}, bf16[1024,128]{1,0:T(8,128)(2,1)}, u32[]{:S(2)}) copy-start(bf16[1024,128]{1,0:T(8,128)(2,1)} %constant.29.clone.refs_5_) | copy-start | bytes 786436
  0.7 35.0 %copy-start.2 = (bf16[4,128,256]{2,1,0:T(8,128)(2,1)S(1)}, bf16[4,128,256]{2,1,0:T(8,128)(2,1)}, u32[]{:S(2)}) copy-start(bf16[4,128,256]{2,1,0:T(8,128)(2,1)} %refs_3_.2) | copy-start | bytes 786436
  0.7 35.0 %copy-start = (bf16[2,4,64,5,1024]{4,2,3,1,0:T(8,128)(2,1)S(1)}, bf16[2,4,64,5,1024]{4,2,3,1,0:T(8,128)(2,1)}, u32[]{:S(2)}) copy-start(bf16[2,4,64,5,1024]{4,2,3,1,0:T(8,128)(2,1)} %param.19) | copy-start | bytes 15728644
  2.9 35.5 %copy-start.3 = (bf16[512,256]{1,0:T(8,128)(2,1)}, bf16[512,256]{1,0:T(8,128)(2,1)S(1)}, u32[]{:S(2)}) copy-start(bf16[512,256]{1,0:T(8,128)(2,1)S(1)} %get-tuple-element.17.refs_1_.grad_hbm) | copy-start | bytes 786436
  51.8 11.6 %all-to-all-start.3 = ((bf16[32,24,128]{2,1,0:T(8,128)(2,1)}), bf16[32,24,128]{2,1,0:T(8,128)(2,1)S(1)}, u32[]{:S(2)}, u32[]{:S(2)}) async-start(bf16[32,24,128]{2,1,0:T(8,128)(2,1)} %bitcast.7), calls=%async_computation.3 | async-start | bytes 393216 | tf_op jit(solution)/shard_map/all_to_all | solution.py:553
  54.1 5.2 %copy-start.6 = (bf16[256,32]{1,0:T(8,128)(2,1)S(1)}, bf16[256,32]{1,0:T(8,128)(2,1)}, u32[]{:S(2)}) copy-start(bf16[256,32]{1,0:T(8,128)(2,1)} %constant.30.clone.spread_ref) | copy-start | bytes 49156
  54.2 5.2 %copy-start.7 = (bf16[32,32]{1,0:T(8,128)(2,1)S(1)}, bf16[32,32]{1,0:T(8,128)(2,1)}, u32[]{:S(2)}) copy-start(bf16[32,32]{1,0:T(8,128)(2,1)} %bypass_ref.1) | copy-start | bytes 6148

commit v4 on v3

--- a/solution.py
+++ b/solution.py
@@ -252,7 +252,7 @@
     return {name: np.asarray(table, np.float32).astype(jnp.bfloat16) for name, table in tables.items()}
 
 
-def call(kernel, out_shapes, *operands, scratch=(), far=(), limit=12, keep=True):
+def call(kernel, out_shapes, *operands, scratch=(), far=(), limit=12, keep=True, away=False):
     near = pl.BlockSpec(memory_space=pltpu.VMEM)
     stay = pl.BlockSpec(memory_space=pltpu.HBM)
     space = lambda i: pltpu.HBM if i in far else pltpu.VMEM
@@ -262,7 +262,7 @@
         kernel,
         out_shape=jax.tree.map(hold, out_shapes),
         in_specs=[stay if i in far else near for i in range(len(operands))],
-        out_specs=jax.tree.map(lambda _: near, out_shapes),
+        out_specs=stay if away else jax.tree.map(lambda _: near, out_shapes),
         scratch_shapes=list(scratch),
         compiler_params=pltpu.CompilerParams(vmem_limit_bytes=limit * 1024 * 1024),
     )(*operands)
@@ -477,7 +477,7 @@
         copy.wait()
 
 
-def rows_back_kernel(in_ref, table_ref, out_ref, *, chans):
+def rows_back_kernel(in_ref, table_ref, out_hbm, out_ref, sems, *, chans):
     re, im, tail = unpack(in_ref[...], 3)
     size = table_ref.shape[1]
     back_cos, back_sin, total = [table_ref[i * size : (i + 1) * size] for i in range(3)]
@@ -487,13 +487,22 @@
     last = last.astype(BF)
     direct = jnp.concatenate([re, im, last], axis=1)
     turned = jnp.concatenate([-im, re, turned_last], axis=1)
-    rows = dot(back_cos, direct) + dot(back_sin, turned)
     summed = dot(total, tail)
     summed = summed + pltpu.roll(summed, LANES - chans, 1)
     summed = jnp.where(group == 2, summed, 0.0)
-    summed = summed + pltpu.roll(summed, chans, 1)
-    re, im, last = lane_blocks(rows)
-    out_ref[...] = pack([re, im, last + halves(summed, chans)])
+    terms = halves(summed + pltpu.roll(summed, chans, 1), chans)
+    copies = []
+    pieces = sems.shape[0]
+    step, long = size // pieces, out_ref.shape[0] // pieces
+    for i in range(pieces):
+        here, there = slice(i * step, (i + 1) * step), slice(i * long, (i + 1) * long)
+        rows = dot(back_cos[here], direct) + dot(back_sin[here], turned)
+        re, im, last = lane_blocks(rows)
+        out_ref[there] = pack([re, im, last + terms[here]])
+        copies.append(pltpu.make_async_copy(out_ref.at[there], out_hbm.at[there], sems.at[i]))
+        copies[i].start()
+    for copy in copies:
+        copy.wait()
 
 
 def columns_back_kernel(in_ref, mixed_ref, first_ref, long_ref, out_ref, bypass_ref, *, factor):
@@ -595,6 +604,9 @@
         lambda *refs: rows_back_kernel(*refs, chans=chans),
         shape((3 * chunk, LANES), BF),
         swap_parts(sent), back_table,
+        keep=False,
+        away=True,
+        scratch=[pltpu.VMEM((3 * chunk, LANES), BF), pltpu.SemaphoreType.DMA((2,))],
     )
     mixed, long, first = call(
         mixing_kernel,

time: 65 us -> 64.8 us (level)
  no operation moved by 1% of the time
where the time goes in v4:
time: 64.8 us; the launch traced here: 64.5 us
  blocking collectives  44.6 us (69%)
  Pallas kernels  14.1 us (22%)
  waiting for transfers between devices  2.66 us (4%)
  starting transfers between devices  2.38 us (4%)
  between operations  0.79 us (1%)
    all_to_all x3, blocking collectives, swap_parts(): return lax.all_to_all(array, 'row', 0, 0, tiled=True)  44.6 us
    pallas_call x6, Pallas kernels, call(): pl.pallas_call(kernel, out_shape=jax.tree.map(hold, out_shapes), in_specs...  8.84 us
    pallas_call x1, Pallas kernels, local(): pl.pallas_call(lambda *refs: weight_kernel(*refs, factor=factor), out_sha...  5.21 us
    all_to_all x1, waiting for transfers between devices, swap_parts(): return lax.all_to_all(array, 'row', 0, 0, tiled=True)  2.66 us
    all_to_all x1, starting transfers between devices, swap_parts(): return lax.all_to_all(array, 'row', 0, 0, tiled=True)  2.38 us
  transfers between devices with their start and end apart: 1, of which 1 were waited for; matrix products, arithmetic and copies ran while one was open for 0% of the time, Pallas kernels for 10%

profile of v4, /device:TPU:1, one launch (start us, length us, event | category | flops | bytes accessed | tf_op | source)
XLA Modules:
  0.0 64.5 jit_solution(15369949672380348409)
XLA Ops:
  0.6 0.0 copy-start.1
  0.6 0.0 copy-start.5
  0.7 0.0 copy-start.4
  0.7 0.0 copy-start.2
  0.7 0.0 copy-start
  0.7 2.2 %shard_map.175 = (bf16[1280,128]{1,0:T(8,128)(2,1)S(1)}, bf16[512,256]{1,0:T(8,128)(2,1)S(1)}, bf16[512,256]{1,0:T(8,128)(2,1)S(1)}) custom-call(bf16[4,128,256]{2,1,0:T(8,128)(2,1)} %refs_3_.2, bf16[4,128,256]{2,1,0:T(8,128)(2,1)} %refs_1_.1, bf16[4,128,256]{2,1,0:T(8,128)(2,1)} %refs_2_.2, bf16[256,256]{1,0:T(8,128)(2,1)} %constant.26.clone.refs_3_, ...), custom_call_target="tpu_custom_call" | custom-call | tf_op jit(solution)/shard_map/pallas_call | solution.py:261
  2.9 0.0 copy-start.3
  2.9 18.2 %all_to_all.44 = bf16[32,40,128]{2,1,0:T(8,128)(2,1)S(1)} all-to-all(bf16[32,40,128]{2,1,0:T(8,128)(2,1)S(1)} %bitcast.17), channel_id=1, replica_groups=mesh['row'=32,'col'=1] {'row'}, dimensions={0} | all-to-all | bytes 655360 | tf_op jit(solution)/shard_map/all_to_all | solution.py:562
  21.1 0.4 shard_map.176
  21.4 14.2 %all_to_all.45 = bf16[32,40,128]{2,1,0:T(8,128)(2,1)S(1)} all-to-all(bf16[32,40,128]{2,1,0:T(8,128)(2,1)S(1)} %bitcast.14), channel_id=1, replica_groups=mesh['row'=32,'col'=1] {'row'}, dimensions={0} | all-to-all | bytes 655360 | tf_op jit(solution)/shard_map/all_to_all | solution.py:562
  35.7 0.0 copy-done.1
  35.7 0.0 copy-done.5
  35.7 0.0 copy-done.4
  35.7 0.0 copy-done.2
  35.7 0.0 copy-done
  35.7 2.7 %shard_map.177 = (bf16[768,128]{1,0:T(8,128)(2,1)S(1)}, bf16[256,640]{1,0:T(8,128)(2,1)S(1)}, bf16[6,128,1024]{2,1,0:T(8,128)(2,1)S(1)}, bf16[768,256]{1,0:T(8,128)(2,1)S(1)}) custom-call(bf16[1280,128]{1,0:T(8,128)(2,1)S(1)} %bitcast.12, bf16[512,256]{1,0:T(8,128)(2,1)S(1)} %get-tuple-element.17.refs_1_.grad_hbm, bf16[2,4,5,64,1024]{4,3,2,1,0:T(8,128)(2,1)S(1)} %bitcast.11, ...), custom_call_target="tpu_custom_call" | custom-call | tf_op jit(solution)/shard_map/pallas_call | solution.py:261
  38.4 0.0 copy-done.3
  38.4 12.2 %all_to_all.46 = bf16[32,24,128]{2,1,0:T(8,128)(2,1)S(1)} all-to-all(bf16[32,24,128]{2,1,0:T(8,128)(2,1)S(1)} %bitcast.18), channel_id=1, replica_groups=mesh['row'=32,'col'=1] {'row'}, dimensions={0} | all-to-all | bytes 393216 | tf_op jit(solution)/shard_map/all_to_all | solution.py:562
  50.5 1.0 %shard_map.178.sent_hbm = bf16[768,128]{1,0:T(8,128)(2,1)} custom-call(bf16[768,128]{1,0:T(8,128)(2,1)S(1)} %bitcast.16, bf16[768,256]{1,0:T(8,128)(2,1)S(1)} %get-tuple-element.19.refs_1_), custom_call_target="tpu_custom_call" | custom-call | tf_op jit(solution)/shard_map/pallas_call | solution.py:261
  51.6 2.4 %all-to-all-start.3 = ((bf16[32,24,128]{2,1,0:T(8,128)(2,1)}), bf16[32,24,128]{2,1,0:T(8,128)(2,1)S(1)}, u32[]{:S(2)}, u32[]{:S(2)}) async-start(bf16[32,24,128]{2,1,0:T(8,128)(2,1)} %bitcast.7), calls=%async_computation.3 | async-start | bytes 393216 | tf_op jit(solution)/shard_map/all_to_all | solution.py:562
  54.0 0.0 copy-start.6
  54.0 0.0 copy-start.7
  54.0 5.2 %shard_map.181 = f32[2,4,5,64,1024]{4,3,2,1,0:T(8,128)} custom-call(bf16[256,640]{1,0:T(8,128)(2,1)S(1)} %get-tuple-element.24.refs_0_, bf16[6,128,1024]{2,1,0:T(8,128)(2,1)S(1)} %get-tuple-element.25.refs_1_, bf16[896,256]{1,0:T(8,128)(2,1)S(1)} %copy-done.1), custom_call_target="tpu_custom_call" | custom-call | tf_op jit(solution)/shard_map/pallas_call | solution.py:593
  59.2 0.0 copy-done.6
  59.2 0.0 copy-done.7
  59.2 1.3 %shard_map.179 = (f32[512,256]{1,0:T(8,128)S(1)}, bf16[896,512]{1,0:T(8,128)(2,1)S(1)}, bf16[32,256]{1,0:T(8,128)(2,1)S(1)}) custom-call(bf16[768,128]{1,0:T(8,128)(2,1)} %shard_map.178.sent_hbm, bf16[512,256]{1,0:T(8,128)(2,1)} %copy-done.3, bf16[896,512]{1,0:T(8,128)(2,1)} %constant.25.clone.long_hbm, bf16[32,256]{1,0:T(8,128)(2,1)} %constant.32.clone.first_hbm, ...), custom_call_target="tpu_custom_call" | custom-call | tf_op jit(solution)/shard_map/pallas_call | solution.py:261
  60.5 2.7 %all-to-all-done.3 = bf16[32,24,128]{2,1,0:T(8,128)(2,1)S(1)} async-done(((bf16[32,24,128]{2,1,0:T(8,128)(2,1)}), bf16[32,24,128]{2,1,0:T(8,128)(2,1)S(1)}, u32[]{:S(2)}, u32[]{:S(2)}) %all-to-all-start.3) | async-done | bytes 196640 | tf_op jit(solution)/shard_map/all_to_all | solution.py:562
  63.2 1.3 %shard_map.180 = (bf16[4,128,256]{2,1,0:T(8,128)(2,1)}, f32[32,32]{1,0:T(8,128)}) custom-call(bf16[768,128]{1,0:T(8,128)(2,1)S(1)} %bitcast.15, f32[512,256]{1,0:T(8,128)S(1)} %get-tuple-element.20.refs_1_, bf16[32,256]{1,0:T(8,128)(2,1)S(1)} %get-tuple-element.21.refs_2_, bf16[896,512]{1,0:T(8,128)(2,1)S(1)} %get-tuple-element.22.refs_3_), custom_call_target="tpu_custom_call" | custom-call | tf_op jit(solution)/shard_map/pallas_call | solution.py:261
Async XLA Ops:
  0.6 35.0 %copy-start.1 = (bf16[896,256]{1,0:T(8,128)(2,1)S(1)}, bf16[896,256]{1,0:T(8,128)(2,1)}, u32[]{:S(2)}) copy-start(bf16[896,256]{1,0:T(8,128)(2,1)} %constant.23.clone.refs_4_.refs_2_) | copy-start | bytes 1376260
  0.6 35.0 %copy-start.5 = (bf16[256,32]{1,0:T(8,128)(2,1)S(1)}, bf16[256,32]{1,0:T(8,128)(2,1)}, u32[]{:S(2)}) copy-start(bf16[256,32]{1,0:T(8,128)(2,1)} %constant.31.clone.refs_6_) | copy-start | bytes 49156
  0.7 35.0 %copy-start.4 = (bf16[1024,128]{1,0:T(8,128)(2,1)S(1)}, bf16[1024,128]{1,0:T(8,128)(2,1)}, u32[]{:S(2)}) copy-start(bf16[1024,128]{1,0:T(8,128)(2,1)} %constant.29.clone.refs_5_) | copy-start | bytes 786436
  0.7 35.0 %copy-start.2 = (bf16[4,128,256]{2,1,0:T(8,128)(2,1)S(1)}, bf16[4,128,256]{2,1,0:T(8,128)(2,1)}, u32[]{:S(2)}) copy-start(bf16[4,128,256]{2,1,0:T(8,128)(2,1)} %refs_3_.2) | copy-start | bytes 786436
  0.7 35.0 %copy-start = (bf16[2,4,64,5,1024]{4,2,3,1,0:T(8,128)(2,1)S(1)}, bf16[2,4,64,5,1024]{4,2,3,1,0:T(8,128)(2,1)}, u32[]{:S(2)}) copy-start(bf16[2,4,64,5,1024]{4,2,3,1,0:T(8,128)(2,1)} %param.19) | copy-start | bytes 15728644
  2.9 35.5 %copy-start.3 = (bf16[512,256]{1,0:T(8,128)(2,1)}, bf16[512,256]{1,0:T(8,128)(2,1)S(1)}, u32[]{:S(2)}) copy-start(bf16[512,256]{1,0:T(8,128)(2,1)S(1)} %get-tuple-element.17.refs_1_.grad_hbm) | copy-start | bytes 786436
  51.6 11.6 %all-to-all-start.3 = ((bf16[32,24,128]{2,1,0:T(8,128)(2,1)}), bf16[32,24,128]{2,1,0:T(8,128)(2,1)S(1)}, u32[]{:S(2)}, u32[]{:S(2)}) async-start(bf16[32,24,128]{2,1,0:T(8,128)(2,1)} %bitcast.7), calls=%async_computation.3 | async-start | bytes 393216 | tf_op jit(solution)/shard_map/all_to_all | solution.py:562
  54.0 5.2 %copy-start.6 = (bf16[256,32]{1,0:T(8,128)(2,1)S(1)}, bf16[256,32]{1,0:T(8,128)(2,1)}, u32[]{:S(2)}) copy-start(bf16[256,32]{1,0:T(8,128)(2,1)} %constant.30.clone.spread_ref) | copy-start | bytes 49156
  54.0 5.2 %copy-start.7 = (bf16[32,32]{1,0:T(8,128)(2,1)S(1)}, bf16[32,32]{1,0:T(8,128)(2,1)}, u32[]{:S(2)}) copy-start(bf16[32,32]{1,0:T(8,128)(2,1)} %bypass_ref.1) | copy-start | bytes 6148

commit v5 on v4

--- a/solution.py
+++ b/solution.py
@@ -262,7 +262,7 @@
         kernel,
         out_shape=jax.tree.map(hold, out_shapes),
         in_specs=[stay if i in far else near for i in range(len(operands))],
-        out_specs=stay if away else jax.tree.map(lambda _: near, out_shapes),
+        out_specs=jax.tree.map(lambda _: stay if away else near, out_shapes),
         scratch_shapes=list(scratch),
         compiler_params=pltpu.CompilerParams(vmem_limit_bytes=limit * 1024 * 1024),
     )(*operands)
@@ -273,14 +273,7 @@
 
 
 def pack(blocks):
-    parts = blocks[0].shape[0] // SUB
-    stacked = jnp.concatenate([b.reshape(parts, SUB, LANES) for b in blocks], axis=1)
-    return stacked.reshape(-1, LANES).astype(BF)
-
-
-def unpack(rows, count):
-    cube = rows.astype(jnp.float32).reshape(-1, count * SUB, LANES)
-    return [cube[:, i * SUB : (i + 1) * SUB].reshape(-1, LANES).astype(BF) for i in range(count)]
+    return jnp.concatenate(blocks, axis=1).astype(BF)
 
 
 def lane_group(shape, chans):
@@ -387,13 +380,13 @@
 
 def rows_kernel(in_ref, square_ref, weight_hbm, out_ref, *, chans):
     del weight_hbm
-    in_re, in_im, gr_re, gr_im, last = unpack(in_ref[...], 5)
+    direct = in_ref[...]
+    in_re, in_im, gr_re, gr_im, last = lane_blocks(direct)
     size = square_ref.shape[1]
     turned_last = quarter_turn(last.astype(jnp.float32), chans).astype(BF)
-    direct = jnp.concatenate([in_re, in_im, gr_re, gr_im, last], axis=1)
     turned = jnp.concatenate([in_im, -in_re, gr_im, -gr_re, turned_last], axis=1)
     modes = dot(square_ref[:size], direct) + dot(square_ref[size : 2 * size], turned)
-    out_ref[...] = pack(lane_blocks(modes))
+    out_ref[...] = modes.astype(BF)
 
 
 def mixing_tables(table_ref):
@@ -410,13 +403,12 @@
     copies = start_copies(sems, (rows_hbm, rows_ref), (repeat_hbm, repeat_ref))
     size = table_ref.shape[1]
     order, unorder, tile_a, tile_b, tile_last = mixing_tables(table_ref)
-    lanes = jnp.concatenate(unpack(in_ref[...], 5), axis=1)
-    modes = dot(order, lanes).astype(BF)
+    modes = dot(order, in_ref[...]).astype(BF)
     modes_ref[...] = modes
     steps = weight_ref.shape[2]
     wide = weight_ref.shape[4]
     lead = LANES // chans
-    gr_re, gr_im, last = lane_blocks(modes)[2:]
+    gr_re, gr_im, last = lane_blocks(modes_ref[...])[2:]
     first = jnp.concatenate([gr_re, gr_im], axis=1)
     blank = jnp.zeros((LANES, LANES), BF)
     tiles = [
@@ -478,7 +470,7 @@
 
 
 def rows_back_kernel(in_ref, table_ref, out_hbm, out_ref, sems, *, chans):
-    re, im, tail = unpack(in_ref[...], 3)
+    re, im, tail = lane_blocks(in_ref[...])
     size = table_ref.shape[1]
     back_cos, back_sin, total = [table_ref[i * size : (i + 1) * size] for i in range(3)]
     group = lane_group(tail.shape, chans)
@@ -505,19 +497,29 @@
         copy.wait()
 
 
-def columns_back_kernel(in_ref, mixed_ref, first_ref, long_ref, out_ref, bypass_ref, *, factor):
+def columns_back_kernel(
+    in_ref, mixed_ref, first_ref, long_ref, out_hbm, bypass_hbm, out_ref, bypass_ref, sems, *, factor
+):
     rows, cols, width = out_ref.shape
     chans = bypass_ref.shape[0]
-    blocks = unpack(in_ref[...], 3)
-    lanes = jnp.concatenate(blocks, axis=1)
+    lanes = in_ref[...]
     height = lanes.shape[1]
     steps = dot(lanes, long_ref[:height]).astype(BF)
-    stacked = jnp.concatenate([steps[:, :width], steps[:, width:]], axis=0)
-    total = dot(long_ref[height:], stacked) + mixed_ref[...]
-    out_ref[...] = total.reshape(rows, cols, width).astype(BF)
-    sums = dot(first_ref[...], blocks[2])
+    sums = dot(first_ref[...], lane_blocks(lanes)[2])
     sums = pltpu.roll(sums + pltpu.roll(sums, LANES - chans, 1), LANES // 2, 1)
     bypass_ref[...] = sums[:, :chans] * factor
+    copies = start_copies(sems, (bypass_ref, bypass_hbm))
+    stacked = jnp.concatenate([steps[:, :width], steps[:, width:]], axis=0)
+    pieces = sems.shape[0] - 1
+    size = rows // pieces
+    for i in range(pieces):
+        here, part = slice(i * size, (i + 1) * size), slice(i * size * cols, (i + 1) * size * cols)
+        turns = long_ref[height + i * size * cols : height + (i + 1) * size * cols]
+        out_ref[here] = (dot(turns, stacked) + mixed_ref[part]).reshape(size, cols, width).astype(BF)
+        copies.append(pltpu.make_async_copy(out_ref.at[here], out_hbm.at[here], sems.at[1 + i]))
+        copies[-1].start()
+    for copy in copies:
+        copy.wait()
 
 
 def local(inputs, preactivation, cotangent, spectral, bypass):
@@ -567,7 +569,7 @@
     field = (rows * cols, width)
     sent, pre_grad, square = call(
         lambda *refs: columns_kernel(*refs, chans=chans),
-        (shape((5 * chunk, LANES), BF), shape(field, BF))
+        (shape((chunk, 5 * LANES), BF), shape(field, BF))
         + (like(square),),
         inputs, preactivation, cotangent, time_table, col_table, square,
         far=range(6),
@@ -577,13 +579,13 @@
     weight = spectral.transpose(0, 1, 3, 2, 4)
     sent = call(
         lambda *refs: rows_kernel(*refs, chans=chans),
-        shape((5 * chunk, LANES), BF),
+        shape((chunk, 5 * LANES), BF),
         swap_parts(sent), square, weight,
         far=(2,),
     )
     sent, modes, repeat, back_table = call(
         lambda *refs: back_kernel(*refs, factor=factor),
-        (shape((3 * chunk, LANES), BF), shape((kept * col_modes, 5 * LANES), BF), like(repeat), like(back_table)),
+        (shape((chunk, 3 * LANES), BF), shape((kept * col_modes, 5 * LANES), BF), like(repeat), like(back_table)),
         swap_parts(sent), pre_grad, weight, inputs, mixing, sums, place, repeat, back_table,
         far=(7, 8),
         scratch=[pltpu.SemaphoreType.DMA((2,))],
@@ -602,11 +604,11 @@
     )(*[pltpu.with_memory_space_constraint(a, pltpu.VMEM) for a in (modes, repeat, mixing)]).transpose(0, 1, 3, 2, 4)
     sent = call(
         lambda *refs: rows_back_kernel(*refs, chans=chans),
-        shape((3 * chunk, LANES), BF),
+        shape((chunk, 3 * LANES), BF),
         swap_parts(sent), back_table,
         keep=False,
         away=True,
-        scratch=[pltpu.VMEM((3 * chunk, LANES), BF), pltpu.SemaphoreType.DMA((2,))],
+        scratch=[pltpu.VMEM((chunk, 3 * LANES), BF), pltpu.SemaphoreType.DMA((2,))],
     )
     mixed, long, first = call(
         mixing_kernel,
@@ -620,6 +622,12 @@
         (shape((rows, cols, width), BF), shape((chans, chans), jnp.float32)),
         swap_parts(sent), mixed, first, long,
         keep=False,
+        away=True,
+        scratch=[
+            pltpu.VMEM((rows, cols, width), BF),
+            pltpu.VMEM((chans, chans), jnp.float32),
+            pltpu.SemaphoreType.DMA((3,)),
+        ],
     )
     return (grad_inputs, grad_spectral, grad_bypass)
 

time: 64.8 us -> 64.7 us (level)
  no operation moved by 1% of the time
where the time goes in v5:
time: 64.7 us; the launch traced here: 64.5 us
  blocking collectives  44.6 us (69%)
  Pallas kernels  14 us (22%)
  waiting for transfers between devices  2.65 us (4%)
  starting transfers between devices  2.38 us (4%)
  between operations  0.79 us (1%)
    all_to_all x3, blocking collectives, swap_parts(): return lax.all_to_all(array, 'row', 0, 0, tiled=True)  44.6 us
    pallas_call x6, Pallas kernels, call(): pl.pallas_call(kernel, out_shape=jax.tree.map(hold, out_shapes), in_specs...  8.84 us
    pallas_call x1, Pallas kernels, local(): pl.pallas_call(lambda *refs: weight_kernel(*refs, factor=factor), out_sha...  5.21 us
    all_to_all x1, waiting for transfers between devices, swap_parts(): return lax.all_to_all(array, 'row', 0, 0, tiled=True)  2.65 us
    all_to_all x1, starting transfers between devices, swap_parts(): return lax.all_to_all(array, 'row', 0, 0, tiled=True)  2.38 us
  transfers between devices with their start and end apart: 1, of which 1 were waited for; matrix products, arithmetic and copies ran while one was open for 0% of the time, Pallas kernels for 10%

profile of v5, /device:TPU:1, one launch (start us, length us, event | category | flops | bytes accessed | tf_op | source)
XLA Modules:
  0.0 64.5 jit_solution(3706175557897117207)
XLA Ops:
  0.6 0.0 copy-start.1
  0.6 0.0 copy-start.5
  0.7 0.0 copy-start.4
  0.7 0.0 copy-start.2
  0.7 0.0 copy-start
  0.7 2.2 %shard_map.175 = (bf16[256,640]{1,0:T(8,128)(2,1)S(1)}, bf16[512,256]{1,0:T(8,128)(2,1)S(1)}, bf16[512,256]{1,0:T(8,128)(2,1)S(1)}) custom-call(bf16[4,128,256]{2,1,0:T(8,128)(2,1)} %refs_3_.2, bf16[4,128,256]{2,1,0:T(8,128)(2,1)} %refs_1_.1, bf16[4,128,256]{2,1,0:T(8,128)(2,1)} %refs_2_.2, bf16[256,256]{1,0:T(8,128)(2,1)} %constant.26.clone.refs_3_, ...), custom_call_target="tpu_custom_call" | custom-call | tf_op jit(solution)/shard_map/pallas_call | solution.py:261
  2.9 0.0 copy-start.3
  2.9 18.2 %all_to_all.44 = bf16[32,8,640]{2,1,0:T(8,128)(2,1)S(1)} all-to-all(bf16[32,8,640]{2,1,0:T(8,128)(2,1)S(1)} %bitcast.17), channel_id=1, replica_groups=mesh['row'=32,'col'=1] {'row'}, dimensions={0} | all-to-all | bytes 655360 | tf_op jit(solution)/shard_map/all_to_all | solution.py:564
  21.1 0.4 shard_map.176
  21.4 14.2 %all_to_all.45 = bf16[32,8,640]{2,1,0:T(8,128)(2,1)S(1)} all-to-all(bf16[32,8,640]{2,1,0:T(8,128)(2,1)S(1)} %bitcast.14), channel_id=1, replica_groups=mesh['row'=32,'col'=1] {'row'}, dimensions={0} | all-to-all | bytes 655360 | tf_op jit(solution)/shard_map/all_to_all | solution.py:564
  35.7 0.0 copy-done.1
  35.7 0.0 copy-done.5
  35.7 0.0 copy-done.4
  35.7 0.0 copy-done.2
  35.7 0.0 copy-done
  35.7 2.7 %shard_map.177 = (bf16[256,384]{1,0:T(8,128)(2,1)S(1)}, bf16[256,640]{1,0:T(8,128)(2,1)S(1)}, bf16[6,128,1024]{2,1,0:T(8,128)(2,1)S(1)}, bf16[768,256]{1,0:T(8,128)(2,1)S(1)}) custom-call(bf16[256,640]{1,0:T(8,128)(2,1)S(1)} %bitcast.12, bf16[512,256]{1,0:T(8,128)(2,1)S(1)} %get-tuple-element.17.refs_1_.grad_hbm, bf16[2,4,5,64,1024]{4,3,2,1,0:T(8,128)(2,1)S(1)} %bitcast.11, ...), custom_call_target="tpu_custom_call" | custom-call | tf_op jit(solution)/shard_map/pallas_call | solution.py:261
  38.4 0.0 copy-done.3
  38.4 12.2 %all_to_all.46 = bf16[32,8,384]{2,1,0:T(8,128)(2,1)S(1)} all-to-all(bf16[32,8,384]{2,1,0:T(8,128)(2,1)S(1)} %bitcast.18), channel_id=1, replica_groups=mesh['row'=32,'col'=1] {'row'}, dimensions={0} | all-to-all | bytes 393216 | tf_op jit(solution)/shard_map/all_to_all | solution.py:564
  50.6 1.0 %shard_map.178.sent_hbm = bf16[256,384]{1,0:T(8,128)(2,1)} custom-call(bf16[256,384]{1,0:T(8,128)(2,1)S(1)} %bitcast.16, bf16[768,256]{1,0:T(8,128)(2,1)S(1)} %get-tuple-element.19.refs_1_), custom_call_target="tpu_custom_call" | custom-call | tf_op jit(solution)/shard_map/pallas_call | solution.py:261
  51.6 2.4 %all-to-all-start.3 = ((bf16[32,8,384]{2,1,0:T(8,128)(2,1)}), bf16[32,8,384]{2,1,0:T(8,128)(2,1)S(1)}, u32[]{:S(2)}, u32[]{:S(2)}) async-start(bf16[32,8,384]{2,1,0:T(8,128)(2,1)} %bitcast.7), calls=%async_computation.3 | async-start | bytes 393216 | tf_op jit(solution)/shard_map/all_to_all | solution.py:564
  54.0 0.0 copy-start.6
  54.0 0.0 copy-start.7
  54.0 5.2 %shard_map.181 = f32[2,4,5,64,1024]{4,3,2,1,0:T(8,128)} custom-call(bf16[256,640]{1,0:T(8,128)(2,1)S(1)} %get-tuple-element.24.refs_0_, bf16[6,128,1024]{2,1,0:T(8,128)(2,1)S(1)} %get-tuple-element.25.refs_1_, bf16[896,256]{1,0:T(8,128)(2,1)S(1)} %copy-done.1), custom_call_target="tpu_custom_call" | custom-call | tf_op jit(solution)/shard_map/pallas_call | solution.py:595
  59.2 0.0 copy-done.6
  59.2 0.0 copy-done.7
  59.2 1.3 %shard_map.179 = (f32[512,256]{1,0:T(8,128)S(1)}, bf16[896,512]{1,0:T(8,128)(2,1)S(1)}, bf16[32,256]{1,0:T(8,128)(2,1)S(1)}) custom-call(bf16[256,384]{1,0:T(8,128)(2,1)} %shard_map.178.sent_hbm, bf16[512,256]{1,0:T(8,128)(2,1)} %copy-done.3, bf16[896,512]{1,0:T(8,128)(2,1)} %constant.25.clone.long_hbm, bf16[32,256]{1,0:T(8,128)(2,1)} %constant.32.clone.first_hbm, ...), custom_call_target="tpu_custom_call" | custom-call | tf_op jit(solution)/shard_map/pallas_call | solution.py:261
  60.5 2.7 %all-to-all-done.3 = bf16[32,8,384]{2,1,0:T(8,128)(2,1)S(1)} async-done(((bf16[32,8,384]{2,1,0:T(8,128)(2,1)}), bf16[32,8,384]{2,1,0:T(8,128)(2,1)S(1)}, u32[]{:S(2)}, u32[]{:S(2)}) %all-to-all-start.3) | async-done | bytes 196640 | tf_op jit(solution)/shard_map/all_to_all | solution.py:564
  63.2 1.3 %shard_map.180 = (bf16[4,128,256]{2,1,0:T(8,128)(2,1)}, f32[32,32]{1,0:T(8,128)}) custom-call(bf16[256,384]{1,0:T(8,128)(2,1)S(1)} %bitcast.15, f32[512,256]{1,0:T(8,128)S(1)} %get-tuple-element.20.refs_1_, bf16[32,256]{1,0:T(8,128)(2,1)S(1)} %get-tuple-element.21.refs_2_, bf16[896,512]{1,0:T(8,128)(2,1)S(1)} %get-tuple-element.22.refs_3_), custom_call_target="tpu_custom_call" | custom-call | tf_op jit(solution)/shard_map/pallas_call | solution.py:261
Async XLA Ops:
  0.6 35.0 %copy-start.1 = (bf16[896,256]{1,0:T(8,128)(2,1)S(1)}, bf16[896,256]{1,0:T(8,128)(2,1)}, u32[]{:S(2)}) copy-start(bf16[896,256]{1,0:T(8,128)(2,1)} %constant.23.clone.refs_4_.refs_2_) | copy-start | bytes 1376260
  0.6 35.0 %copy-start.5 = (bf16[256,32]{1,0:T(8,128)(2,1)S(1)}, bf16[256,32]{1,0:T(8,128)(2,1)}, u32[]{:S(2)}) copy-start(bf16[256,32]{1,0:T(8,128)(2,1)} %constant.31.clone.refs_6_) | copy-start | bytes 49156
  0.7 35.0 %copy-start.4 = (bf16[1024,128]{1,0:T(8,128)(2,1)S(1)}, bf16[1024,128]{1,0:T(8,128)(2,1)}, u32[]{:S(2)}) copy-start(bf16[1024,128]{1,0:T(8,128)(2,1)} %constant.29.clone.refs_5_) | copy-start | bytes 786436
  0.7 35.0 %copy-start.2 = (bf16[4,128,256]{2,1,0:T(8,128)(2,1)S(1)}, bf16[4,128,256]{2,1,0:T(8,128)(2,1)}, u32[]{:S(2)}) copy-start(bf16[4,128,256]{2,1,0:T(8,128)(2,1)} %refs_3_.2) | copy-start | bytes 786436
  0.7 35.0 %copy-start = (bf16[2,4,64,5,1024]{4,2,3,1,0:T(8,128)(2,1)S(1)}, bf16[2,4,64,5,1024]{4,2,3,1,0:T(8,128)(2,1)}, u32[]{:S(2)}) copy-start(bf16[2,4,64,5,1024]{4,2,3,1,0:T(8,128)(2,1)} %param.19) | copy-start | bytes 15728644
  2.9 35.5 %copy-start.3 = (bf16[512,256]{1,0:T(8,128)(2,1)}, bf16[512,256]{1,0:T(8,128)(2,1)S(1)}, u32[]{:S(2)}) copy-start(bf16[512,256]{1,0:T(8,128)(2,1)S(1)} %get-tuple-element.17.refs_1_.grad_hbm) | copy-start | bytes 786436
  51.6 11.6 %all-to-all-start.3 = ((bf16[32,8,384]{2,1,0:T(8,128)(2,1)}), bf16[32,8,384]{2,1,0:T(8,128)(2,1)S(1)}, u32[]{:S(2)}, u32[]{:S(2)}) async-start(bf16[32,8,384]{2,1,0:T(8,128)(2,1)} %bitcast.7), calls=%async_computation.3 | async-start | bytes 393216 | tf_op jit(solution)/shard_map/all_to_all | solution.py:564
  54.0 5.2 %copy-start.6 = (bf16[256,32]{1,0:T(8,128)(2,1)S(1)}, bf16[256,32]{1,0:T(8,128)(2,1)}, u32[]{:S(2)}) copy-start(bf16[256,32]{1,0:T(8,128)(2,1)} %constant.30.clone.spread_ref) | copy-start | bytes 49156
  54.0 5.2 %copy-start.7 = (bf16[32,32]{1,0:T(8,128)(2,1)S(1)}, bf16[32,32]{1,0:T(8,128)(2,1)}, u32[]{:S(2)}) copy-start(bf16[32,32]{1,0:T(8,128)(2,1)} %bypass_ref.1) | copy-start | bytes 6148

commit v6 on v5

--- a/solution.py
+++ b/solution.py
@@ -385,7 +385,8 @@
     size = square_ref.shape[1]
     turned_last = quarter_turn(last.astype(jnp.float32), chans).astype(BF)
     turned = jnp.concatenate([in_im, -in_re, gr_im, -gr_re, turned_last], axis=1)
-    modes = dot(square_ref[:size], direct) + dot(square_ref[size : 2 * size], turned)
+    phases = jnp.concatenate([square_ref[:size], square_ref[size : 2 * size]], axis=1)
+    modes = dot(phases, jnp.concatenate([direct, turned], axis=0))
     out_ref[...] = modes.astype(BF)
 
 
@@ -483,12 +484,13 @@
     summed = summed + pltpu.roll(summed, LANES - chans, 1)
     summed = jnp.where(group == 2, summed, 0.0)
     terms = halves(summed + pltpu.roll(summed, chans, 1), chans)
+    both = jnp.concatenate([direct, turned], axis=0)
     copies = []
     pieces = sems.shape[0]
     step, long = size // pieces, out_ref.shape[0] // pieces
     for i in range(pieces):
         here, there = slice(i * step, (i + 1) * step), slice(i * long, (i + 1) * long)
-        rows = dot(back_cos[here], direct) + dot(back_sin[here], turned)
+        rows = dot(jnp.concatenate([back_cos[here], back_sin[here]], axis=1), both)
         re, im, last = lane_blocks(rows)
         out_ref[there] = pack([re, im, last + terms[here]])
         copies.append(pltpu.make_async_copy(out_ref.at[there], out_hbm.at[there], sems.at[i]))

time: 64.7 us -> 64.7 us (level)
  no operation moved by 1% of the time
where the time goes in v6:
time: 64.7 us; the launch traced here: 64.5 us
  blocking collectives  44.6 us (69%)
  Pallas kernels  14 us (22%)
  waiting for transfers between devices  2.66 us (4%)
  starting transfers between devices  2.38 us (4%)
  between operations  0.79 us (1%)
    all_to_all x3, blocking collectives, swap_parts(): return lax.all_to_all(array, 'row', 0, 0, tiled=True)  44.6 us
    pallas_call x6, Pallas kernels, call(): pl.pallas_call(kernel, out_shape=jax.tree.map(hold, out_shapes), in_specs...  8.83 us
    pallas_call x1, Pallas kernels, local(): pl.pallas_call(lambda *refs: weight_kernel(*refs, factor=factor), out_sha...  5.2 us
    all_to_all x1, waiting for transfers between devices, swap_parts(): return lax.all_to_all(array, 'row', 0, 0, tiled=True)  2.66 us
    all_to_all x1, starting transfers between devices, swap_parts(): return lax.all_to_all(array, 'row', 0, 0, tiled=True)  2.38 us
  transfers between devices with their start and end apart: 1, of which 1 were waited for; matrix products, arithmetic and copies ran while one was open for 0% of the time, Pallas kernels for 10%

profile of v6, /device:TPU:1, one launch (start us, length us, event | category | flops | bytes accessed | tf_op | source)
XLA Modules:
  0.0 64.5 jit_solution(3005775896352989712)
XLA Ops:
  0.6 0.0 copy-start.1
  0.6 0.0 copy-start.5
  0.7 0.0 copy-start.4
  0.7 0.0 copy-start.2
  0.7 0.0 copy-start
  0.7 2.2 %shard_map.175 = (bf16[256,640]{1,0:T(8,128)(2,1)S(1)}, bf16[512,256]{1,0:T(8,128)(2,1)S(1)}, bf16[512,256]{1,0:T(8,128)(2,1)S(1)}) custom-call(bf16[4,128,256]{2,1,0:T(8,128)(2,1)} %refs_3_.2, bf16[4,128,256]{2,1,0:T(8,128)(2,1)} %refs_1_.1, bf16[4,128,256]{2,1,0:T(8,128)(2,1)} %refs_2_.2, bf16[256,256]{1,0:T(8,128)(2,1)} %constant.26.clone.refs_3_, ...), custom_call_target="tpu_custom_call" | custom-call | tf_op jit(solution)/shard_map/pallas_call | solution.py:261
  2.9 0.0 copy-start.3
  2.9 18.2 %all_to_all.44 = bf16[32,8,640]{2,1,0:T(8,128)(2,1)S(1)} all-to-all(bf16[32,8,640]{2,1,0:T(8,128)(2,1)S(1)} %bitcast.17), channel_id=1, replica_groups=mesh['row'=32,'col'=1] {'row'}, dimensions={0} | all-to-all | bytes 655360 | tf_op jit(solution)/shard_map/all_to_all | solution.py:566
  21.1 0.4 shard_map.176
  21.4 14.2 %all_to_all.45 = bf16[32,8,640]{2,1,0:T(8,128)(2,1)S(1)} all-to-all(bf16[32,8,640]{2,1,0:T(8,128)(2,1)S(1)} %bitcast.14), channel_id=1, replica_groups=mesh['row'=32,'col'=1] {'row'}, dimensions={0} | all-to-all | bytes 655360 | tf_op jit(solution)/shard_map/all_to_all | solution.py:566
  35.7 0.0 copy-done.1
  35.7 0.0 copy-done.5
  35.7 0.0 copy-done.4
  35.7 0.0 copy-done.2
  35.7 0.0 copy-done
  35.7 2.7 %shard_map.177 = (bf16[256,384]{1,0:T(8,128)(2,1)S(1)}, bf16[256,640]{1,0:T(8,128)(2,1)S(1)}, bf16[6,128,1024]{2,1,0:T(8,128)(2,1)S(1)}, bf16[768,256]{1,0:T(8,128)(2,1)S(1)}) custom-call(bf16[256,640]{1,0:T(8,128)(2,1)S(1)} %bitcast.12, bf16[512,256]{1,0:T(8,128)(2,1)S(1)} %get-tuple-element.17.refs_1_.grad_hbm, bf16[2,4,5,64,1024]{4,3,2,1,0:T(8,128)(2,1)S(1)} %bitcast.11, ...), custom_call_target="tpu_custom_call" | custom-call | tf_op jit(solution)/shard_map/pallas_call | solution.py:261
  38.4 0.0 copy-done.3
  38.4 12.2 %all_to_all.46 = bf16[32,8,384]{2,1,0:T(8,128)(2,1)S(1)} all-to-all(bf16[32,8,384]{2,1,0:T(8,128)(2,1)S(1)} %bitcast.18), channel_id=1, replica_groups=mesh['row'=32,'col'=1] {'row'}, dimensions={0} | all-to-all | bytes 393216 | tf_op jit(solution)/shard_map/all_to_all | solution.py:566
  50.6 1.0 %shard_map.178.sent_hbm = bf16[256,384]{1,0:T(8,128)(2,1)} custom-call(bf16[256,384]{1,0:T(8,128)(2,1)S(1)} %bitcast.16, bf16[768,256]{1,0:T(8,128)(2,1)S(1)} %get-tuple-element.19.refs_1_), custom_call_target="tpu_custom_call" | custom-call | tf_op jit(solution)/shard_map/pallas_call | solution.py:261
  51.6 2.4 %all-to-all-start.3 = ((bf16[32,8,384]{2,1,0:T(8,128)(2,1)}), bf16[32,8,384]{2,1,0:T(8,128)(2,1)S(1)}, u32[]{:S(2)}, u32[]{:S(2)}) async-start(bf16[32,8,384]{2,1,0:T(8,128)(2,1)} %bitcast.7), calls=%async_computation.3 | async-start | bytes 393216 | tf_op jit(solution)/shard_map/all_to_all | solution.py:566
  54.0 0.0 copy-start.6
  54.0 0.0 copy-start.7
  54.0 5.2 %shard_map.181 = f32[2,4,5,64,1024]{4,3,2,1,0:T(8,128)} custom-call(bf16[256,640]{1,0:T(8,128)(2,1)S(1)} %get-tuple-element.24.refs_0_, bf16[6,128,1024]{2,1,0:T(8,128)(2,1)S(1)} %get-tuple-element.25.refs_1_, bf16[896,256]{1,0:T(8,128)(2,1)S(1)} %copy-done.1), custom_call_target="tpu_custom_call" | custom-call | tf_op jit(solution)/shard_map/pallas_call | solution.py:597
  59.2 0.0 copy-done.6
  59.2 0.0 copy-done.7
  59.2 1.3 %shard_map.179 = (f32[512,256]{1,0:T(8,128)S(1)}, bf16[896,512]{1,0:T(8,128)(2,1)S(1)}, bf16[32,256]{1,0:T(8,128)(2,1)S(1)}) custom-call(bf16[256,384]{1,0:T(8,128)(2,1)} %shard_map.178.sent_hbm, bf16[512,256]{1,0:T(8,128)(2,1)} %copy-done.3, bf16[896,512]{1,0:T(8,128)(2,1)} %constant.25.clone.long_hbm, bf16[32,256]{1,0:T(8,128)(2,1)} %constant.32.clone.first_hbm, ...), custom_call_target="tpu_custom_call" | custom-call | tf_op jit(solution)/shard_map/pallas_call | solution.py:261
  60.5 2.7 %all-to-all-done.3 = bf16[32,8,384]{2,1,0:T(8,128)(2,1)S(1)} async-done(((bf16[32,8,384]{2,1,0:T(8,128)(2,1)}), bf16[32,8,384]{2,1,0:T(8,128)(2,1)S(1)}, u32[]{:S(2)}, u32[]{:S(2)}) %all-to-all-start.3) | async-done | bytes 196640 | tf_op jit(solution)/shard_map/all_to_all | solution.py:566
  63.2 1.3 %shard_map.180 = (bf16[4,128,256]{2,1,0:T(8,128)(2,1)}, f32[32,32]{1,0:T(8,128)}) custom-call(bf16[256,384]{1,0:T(8,128)(2,1)S(1)} %bitcast.15, f32[512,256]{1,0:T(8,128)S(1)} %get-tuple-element.20.refs_1_, bf16[32,256]{1,0:T(8,128)(2,1)S(1)} %get-tuple-element.21.refs_2_, bf16[896,512]{1,0:T(8,128)(2,1)S(1)} %get-tuple-element.22.refs_3_), custom_call_target="tpu_custom_call" | custom-call | tf_op jit(solution)/shard_map/pallas_call | solution.py:261
Async XLA Ops:
  0.6 35.0 %copy-start.1 = (bf16[896,256]{1,0:T(8,128)(2,1)S(1)}, bf16[896,256]{1,0:T(8,128)(2,1)}, u32[]{:S(2)}) copy-start(bf16[896,256]{1,0:T(8,128)(2,1)} %constant.23.clone.refs_4_.refs_2_) | copy-start | bytes 1376260
  0.6 35.0 %copy-start.5 = (bf16[256,32]{1,0:T(8,128)(2,1)S(1)}, bf16[256,32]{1,0:T(8,128)(2,1)}, u32[]{:S(2)}) copy-start(bf16[256,32]{1,0:T(8,128)(2,1)} %constant.31.clone.refs_6_) | copy-start | bytes 49156
  0.7 35.0 %copy-start.4 = (bf16[1024,128]{1,0:T(8,128)(2,1)S(1)}, bf16[1024,128]{1,0:T(8,128)(2,1)}, u32[]{:S(2)}) copy-start(bf16[1024,128]{1,0:T(8,128)(2,1)} %constant.29.clone.refs_5_) | copy-start | bytes 786436
  0.7 35.0 %copy-start.2 = (bf16[4,128,256]{2,1,0:T(8,128)(2,1)S(1)}, bf16[4,128,256]{2,1,0:T(8,128)(2,1)}, u32[]{:S(2)}) copy-start(bf16[4,128,256]{2,1,0:T(8,128)(2,1)} %refs_3_.2) | copy-start | bytes 786436
  0.7 35.0 %copy-start = (bf16[2,4,64,5,1024]{4,2,3,1,0:T(8,128)(2,1)S(1)}, bf16[2,4,64,5,1024]{4,2,3,1,0:T(8,128)(2,1)}, u32[]{:S(2)}) copy-start(bf16[2,4,64,5,1024]{4,2,3,1,0:T(8,128)(2,1)} %param.19) | copy-start | bytes 15728644
  2.9 35.5 %copy-start.3 = (bf16[512,256]{1,0:T(8,128)(2,1)}, bf16[512,256]{1,0:T(8,128)(2,1)S(1)}, u32[]{:S(2)}) copy-start(bf16[512,256]{1,0:T(8,128)(2,1)S(1)} %get-tuple-element.17.refs_1_.grad_hbm) | copy-start | bytes 786436
  51.6 11.6 %all-to-all-start.3 = ((bf16[32,8,384]{2,1,0:T(8,128)(2,1)}), bf16[32,8,384]{2,1,0:T(8,128)(2,1)S(1)}, u32[]{:S(2)}, u32[]{:S(2)}) async-start(bf16[32,8,384]{2,1,0:T(8,128)(2,1)} %bitcast.7), calls=%async_computation.3 | async-start | bytes 393216 | tf_op jit(solution)/shard_map/all_to_all | solution.py:566
  54.0 5.2 %copy-start.6 = (bf16[256,32]{1,0:T(8,128)(2,1)S(1)}, bf16[256,32]{1,0:T(8,128)(2,1)}, u32[]{:S(2)}) copy-start(bf16[256,32]{1,0:T(8,128)(2,1)} %constant.30.clone.spread_ref) | copy-start | bytes 49156
  54.0 5.2 %copy-start.7 = (bf16[32,32]{1,0:T(8,128)(2,1)S(1)}, bf16[32,32]{1,0:T(8,128)(2,1)}, u32[]{:S(2)}) copy-start(bf16[32,32]{1,0:T(8,128)(2,1)} %bypass_ref.1) | copy-start | bytes 6148
